TPU v7x, 256 devices: a whole 4x4x8 slice. The times are simulated.
256 devices in a mesh: shot: 32 (over x_lo, z, core), freq: 8 (over x_hi, y).
Axes of the slice: x: 4 (x_hi: 2, x_lo: 2; x = x_hi * 2 + x_lo), y: 4, z: 8, core: 2. Of those that a mesh axis runs over, the one named last changes fastest.
Arguments:
- wavefield: bfloat16 [2, 16, 4096, 4096], P(None, 'freq', 'shot'), may hold values from -0.75 to 0.75
- wavelet: float32 [2, 16], P(None, 'freq'), may hold values from -3 to 3
- shot_owner: int32 [4096, 1], P('shot'), may hold values from 0 to 31; in each aligned block of 128 rows (0 to 127, 128 to 255, ...) at most 8 rows name the same one
- trace_map: int32 [4096, 512], P('shot'), may hold values from 0 to 511, each once within a row
Outputs:
- multiples: bfloat16 [32, 8192, 512], P('freq', 'shot')
Inputs may be any that keep to these rules, and one draw needn't show every extreme that they name: `shot_owner`: among the 128 shots of one device no owner is named more than 8 times, and in some device one owner is named exactly 8 times. `trace_map`: each row is a permutation of the 512 window receivers.
All inputs are finite; a program needn't handle non-finite values.
Results may differ from a plain program's by a relative error of at most 0.017.
Values may be sent and summed in bfloat16 or wider, within the bound.
No kernel may reach another device: no remote copies, remote signals or barrier semaphores. Data moves between devices by JAX's collectives and lax.ppermute only.
A program may use at most 64 MiB of HBM per device.

v0:
```python
import math

import jax
import jax.numpy as jnp
from jax import lax
from jax.sharding import PartitionSpec as P


def wave_tables(time_index, freq_index, freq_total):
    phase_turns = (freq_index[None, :] + 1) * time_index[:, None] % (2 * freq_total)
    angles = phase_turns.astype(jnp.float32) * (jnp.pi / freq_total)
    return (jnp.cos(angles) / freq_total, jnp.sin(angles) / freq_total)


def product(leading_factor, trailing_factor):
    return jnp.einsum(
        "mwh,mhc->mwc", leading_factor, trailing_factor, preferred_element_type=jnp.float32
    )


def permute_traces(recorded_wiggles, trace_map):
    shot_count = trace_map.shape[0]
    window = trace_map.shape[1]
    block_shots = math.gcd(shot_count, 16)
    block_total = shot_count // block_shots
    receiver_index = jnp.arange(window, dtype=jnp.int32)

    def one_block(block_index):
        first_shot = block_index * block_shots
        wiggle_block = lax.dynamic_slice_in_dim(recorded_wiggles, first_shot, block_shots, 1)
        map_block = lax.dynamic_slice_in_dim(trace_map, first_shot, block_shots, 0)
        selector = (map_block[:, None, :] == receiver_index[None, :, None]).astype(jnp.bfloat16)
        picked = jnp.einsum(
            "tbr,brj->tbj", wiggle_block, selector, preferred_element_type=jnp.float32
        )
        return picked.astype(jnp.bfloat16)

    blocks = lax.map(one_block, jnp.arange(block_total, dtype=jnp.int32))
    time_rows = recorded_wiggles.shape[0]
    return jnp.transpose(blocks, (1, 0, 2, 3)).reshape(time_rows, shot_count, window)


def shards(wavefield, wavelet, shot_owner, trace_map):
    cutoff_hertz_bin = lax.Precision.HIGHEST
    freq_count = wavefield.shape[1]
    shot_count = wavefield.shape[2]
    window = trace_map.shape[1]
    columns = wavefield[:, :, :, :window]
    incoming = lax.all_gather(columns, "shot", axis=2, tiled=True)
    inphase_entry = product(wavefield[0], incoming[0]) - product(wavefield[1], incoming[1])
    quadrature_entry = product(wavefield[0], incoming[1]) + product(wavefield[1], incoming[0])
    inphase_entry, quadrature_entry = (inphase_entry, quadrature_entry)
    inphase_weight = wavelet[0][:, None, None]
    quadrature_weight = wavelet[1][:, None, None]
    estimate_inphase = (
        inphase_entry * inphase_weight - quadrature_entry * quadrature_weight
    ).astype(jnp.bfloat16)
    estimate_quadrature = (
        inphase_entry * quadrature_weight + quadrature_entry * inphase_weight
    ).astype(jnp.bfloat16)
    estimate_inphase, estimate_quadrature = lax.optimization_barrier(
        (estimate_inphase, estimate_quadrature)
    )
    inphase_fourier = estimate_inphase.astype(jnp.float32)
    quadrature_fourier = estimate_quadrature.astype(jnp.float32)
    freq_total = freq_count * lax.axis_size("freq")
    local_freqs = lax.axis_index("freq") * freq_count + jnp.arange(freq_count, dtype=jnp.int32)
    time_index = jnp.arange(lax.axis_size("freq") * (2 * freq_count), dtype=jnp.int32)
    even_basis_table, odd_basis_table = wave_tables(time_index, local_freqs, freq_total)
    accumulated_sum = jnp.einsum(
        "vq,qjl->vjl", even_basis_table, inphase_fourier, precision=cutoff_hertz_bin
    )
    recorded_wiggles = lax.psum_scatter(
        (
            accumulated_sum
            - jnp.einsum(
                "vq,qjl->vjl", odd_basis_table, quadrature_fourier, precision=cutoff_hertz_bin
            )
        ).astype(jnp.bfloat16),
        "freq",
        scatter_dimension=0,
        tiled=True,
    )
    arranged = permute_traces(recorded_wiggles, trace_map)
    owners = shot_owner[:, 0]
    groups = lax.axis_size("shot")
    capacity = max(2, 2 * shot_count // groups)
    owner_marks = (owners[:, None] == jnp.arange(groups, dtype=jnp.int32)[None, :]).astype(
        jnp.float32
    )
    position = jnp.arange(shot_count, dtype=jnp.int32)
    earlier_mask = (position[:, None] > position[None, :]).astype(jnp.float32)
    earlier = jnp.dot(earlier_mask, owner_marks, precision=cutoff_hertz_bin)
    rank_within = jnp.sum(earlier * owner_marks, axis=1).astype(jnp.int32)
    slot_index = owners * capacity + rank_within
    slot_marks = (
        slot_index[None, :] == jnp.arange(groups * capacity, dtype=jnp.int32)[:, None]
    ).astype(jnp.bfloat16)
    outgoing = jnp.einsum(
        "ps,tsj->tpj", slot_marks, arranged, preferred_element_type=jnp.float32
    ).astype(jnp.bfloat16)
    return lax.all_to_all(outgoing, "shot", split_axis=1, concat_axis=1, tiled=True)


def solution(mesh):
    placed = (P(None, "freq", "shot", None), P(None, "freq"), P("shot", None), P("shot", None))
    return jax.shard_map(
        shards, mesh=mesh, in_specs=placed, out_specs=P("freq", "shot", None), check_vma=False
    )
```

profile of v0, /device:TPU:1, one launch (start us, length us, event | category | flops | bytes accessed | tf_op | source)
XLA Modules:
  0.0 319.7 jit_solution(1580467503518100573)
XLA Ops:
  6.5 1.9 slice.26
  8.5 0.8 slice_bitcast_fusion.11
  9.3 104.0 %all-gather.2.cloned.1.call-done = bf16[2,2,4096,512]{3,2,1,0:T(8,128)(2,1)} async-done(((bf16[2,2,128,512]{3,2,1,0:T(8,128)(2,1)}), bf16[2,2,4096,512]{3,2,1,0:T(8,128)(2,1)}) %all-gather.2.cloned.1.call-update) | async-done | bytes 16777232 | tf_op jit(solution)/shard_map/all_gather | solution.py:49
  113.2 5.4 %fusion.9 = f32[2,128,512]{2,1,0:T(8,128)S(1)} fusion(bf16[2,2,4096,512]{3,2,1,0:T(8,128)(2,1)} %all-gather.2.cloned.1.call-done, bf16[2,2,128,4096]{3,2,1,0:T(8,128)(2,1)} %param.6), kind=kOutput, calls=%fused_computation.14 | convolution fusion | flops 1073741824 | bytes 11010048 | tf_op jit(solution)/shard_map/mwh,mhc->mwc/dot_general | solution.py:16
  118.7 5.4 %fusion.8 = f32[2,128,512]{2,1,0:T(8,128)S(1)} fusion(bf16[2,2,4096,512]{3,2,1,0:T(8,128)(2,1)} %all-gather.2.cloned.1.call-done, bf16[2,2,128,4096]{3,2,1,0:T(8,128)(2,1)S(1)} %copy-done), kind=kOutput, calls=%fused_computation.13 | convolution fusion | flops 1073741824 | bytes 11010048 | tf_op jit(solution)/shard_map/mwh,mhc->mwc/dot_general | solution.py:16
  124.7 1.2 slice-done.3
  125.9 1.5 fusion.21
  127.4 1.5 add_convert_fusion
  128.9 3.6 %fusion.30 = f32[32,128,512]{2,0,1:T(8,128)S(1)} fusion(bf16[2,128,512]{2,1,0:T(8,128)(2,1)S(1)} %get-tuple-element.39, s32[2]{0:T(128)S(1)} %add_add_fusion), kind=kOutput, calls=%fused_computation.35 | convolution fusion | flops 50332608 | bytes 8650760 | tf_op jit(solution)/shard_map/vq,qjl->vjl/dot_general | solution.py:70
  132.5 4.4 %subtract_convert_fusion = bf16[32,128,512]{2,0,1:T(8,128)(2,1)S(1)} fusion(f32[32,128,512]{2,0,1:T(8,128)S(1)} %fusion.30, bf16[2,128,512]{2,1,0:T(8,128)(2,1)S(1)} %get-tuple-element.40, s32[2]{0:T(128)S(1)} %add_add_fusion), kind=kOutput, calls=%fused_computation.12 | convolution fusion | flops 54526912 | bytes 12845064 | tf_op jit(solution)/shard_map/vq,qjl->vjl/dot_general | solution.py:76
  136.9 4.3 %copy.18 = bf16[32,128,512]{2,1,0:T(8,128)(2,1)} copy(bf16[32,128,512]{2,0,1:T(8,128)(2,1)S(1)} %subtract_convert_fusion) | data formatting | bytes 8388608 | tf_op jit(solution)/shard_map/convert_element_type | solution.py:79
  141.5 88.6 %reduce-scatter.2.cloned.1.call-done = bf16[4,128,512]{2,1,0:T(8,128)(2,1)} async-done(((bf16[32,128,512]{2,1,0:T(8,128)(2,1)}), bf16[4,128,512]{2,1,0:T(8,128)(2,1)}) %reduce-scatter.2.cloned.1.call-update) | async-done | bytes 524304 | tf_op jit(solution)/shard_map/reduce_scatter | solution.py:73
  230.1 45.0 %while.11 = (s32[]{:T(128)}, bf16[8,4,16,512]{3,1,2,0:T(4,128)(2,1)S(1)}, s32[8]{0:T(128)S(1)}, s32[128,512]{1,0:T(8,128)}, bf16[4,128,512]{2,1,0:T(8,128)(2,1)}...) while((s32[]{:T(128)}, bf16[8,4,16,512]{3,1,2,0:T(4,128)(2,1)S(1)}, s32[8]{0:T(128)S(1)}, ...), condition=%wide.region_2.3_spmd.clone, body=%wide.region_1.2_spmd.clone.sunk | while | flops 37781508 | bytes 360611 | solution.py:38
  231.2 0.9 constant_dynamic-slice_fusion.5
  232.9 2.9 fusion.62
  236.9 0.9 constant_dynamic-slice_fusion.5
  238.5 2.9 fusion.62
  242.5 0.9 constant_dynamic-slice_fusion.5
  244.1 2.9 fusion.62
  248.1 0.9 constant_dynamic-slice_fusion.5
  249.7 2.9 fusion.62
  253.8 0.9 constant_dynamic-slice_fusion.5
  255.4 2.9 fusion.62
  259.4 0.9 constant_dynamic-slice_fusion.5
  261.0 2.9 fusion.62
  265.0 0.9 constant_dynamic-slice_fusion.5
  266.6 2.9 fusion.62
  270.6 0.9 constant_dynamic-slice_fusion.5
  272.3 2.9 fusion.62
  275.6 1.0 copy.21
  276.6 35.1 %all_to_all.5 = bf16[4,256,512]{2,0,1:T(4,128)(2,1)S(1)} all-to-all(bf16[4,256,512]{2,0,1:T(4,128)(2,1)S(1)} %copy.21), channel_id=1, replica_groups=mesh['shot'=32,'freq'=8] {'shot'}, dimensions={1} | all-to-all | bytes 2097152 | tf_op jit(solution)/shard_map/all_to_all | solution.py:102
  311.7 1.2 copy.22
  (38 shorter events, 12.1 us)
Async XLA Ops:
  6.5 106.7 %all-gather.2.cloned.1.call-start = ((), (), s32[]{:S(2)}) async-start(), calls=%async_computation.2 | async-start | bytes 17301504 | tf_op jit(solution)/shard_map/all_gather | solution.py:49
  8.4 221.7 %reduce-scatter.2.cloned.1.call-start = ((), (), s32[]{:S(2)}) async-start(), calls=%async_computation.3 | async-start | bytes 4718592 | tf_op jit(solution)/shard_map/reduce_scatter | solution.py:73
  113.2 5.4 %copy-start = (bf16[2,2,128,4096]{3,2,1,0:T(8,128)(2,1)S(1)}, bf16[2,2,128,4096]{3,2,1,0:T(8,128)(2,1)}, u32[]{:S(2)}) copy-start(bf16[2,2,128,4096]{3,2,1,0:T(8,128)(2,1)} %param.6) | copy-start | bytes 12582916
  113.2 10.9 %slice-start = ((s8[16777216]{0:T(1024)(128)(4,1)}), s8[4194304]{0:T(1024)(128)(4,1)S(1)}, s32[]{:S(2)}) async-start(s8[16777216]{0:T(1024)(128)(4,1)} %bitcast.62), calls=%async_computation.4 | async-start | bytes 8388608
  113.2 10.9 %slice-start.1 = ((s8[16777216]{0:T(1024)(128)(4,1)}), s8[4194304]{0:T(1024)(128)(4,1)S(1)}, s32[]{:S(2)}) async-start(s8[16777216]{0:T(1024)(128)(4,1)} %bitcast.62), calls=%async_computation.5 | async-start | bytes 8388608
  118.7 6.0 %slice-start.2 = ((s8[16777216]{0:T(1024)(128)(4,1)}), s8[4194304]{0:T(1024)(128)(4,1)S(1)}, s32[]{:S(2)}) async-start(s8[16777216]{0:T(1024)(128)(4,1)} %bitcast.62), calls=%async_computation.6 | async-start | bytes 8388608
  118.7 7.2 %slice-start.3 = ((s8[16777216]{0:T(1024)(128)(4,1)}), s8[4194304]{0:T(1024)(128)(4,1)S(1)}, s32[]{:S(2)}) async-start(s8[16777216]{0:T(1024)(128)(4,1)} %bitcast.62), calls=%async_computation.7 | async-start | bytes 8388608
  136.9 4.4 %copy-start.1 = (s32[128,1]{0,1:T(1,128)S(1)}, s32[128,1]{0,1:T(1,128)}, u32[]{:S(2)}) copy-start(s32[128,1]{0,1:T(1,128)} %param.8) | copy-start | bytes 1540
Sparse Core Ops, SparseCore 0:
  9.2 103.9 all-gather.1
  141.4 88.6 reduce-scatter.1
where the time goes:
time: 322 us; the launch traced here: 320 us
  waiting for transfers between devices  193 us (60%)
  matrix products  45.3 us (14%)
  blocking collectives  35.1 us (11%)
  local copies, waits for them, and re-layouts  28.5 us (9%)
  between operations  13.5 us (4%)
  loops' own time  4.59 us (1%)
    all_gather x1, waiting for transfers between devices, shards(): incoming = lax.all_gather(columns, 'shot', axis=2, tiled=True)  104 us
    reduce_scatter x1, waiting for transfers between devices, shards(): lax.psum_scatter((accumulated_sum - jnp.einsum('vq,qjl->vjl', odd_basis_t...  88.6 us
    all_to_all x1, blocking collectives, shards(): lax.all_to_all(outgoing, 'shot', split_axis=1, concat_axis=1, tiled=True)  35.1 us
    dot_general x8, matrix products, one_block(): jnp.einsum('tbr,brj->tbj', wiggle_block, selector, preferred_element_type...  22.8 us
    dot_general x4, matrix products, product(): jnp.einsum('mwh,mhc->mwc', leading_factor, trailing_factor, preferred_ele...  13.9 us
    dynamic_slice x8, local copies, waits for them, and re-layouts, one_block(): lax.dynamic_slice_in_dim(recorded_wiggles, first_shot, block_shots, 1)  6.83 us
  transfers between devices with their start and end apart: 2, of which 2 were waited for; matrix products, arithmetic and copies ran while one was open for 0% of the time, Pallas kernels for 0%

commit v1 on v0

v1 whole, which is shorter than its diff:
```python
import jax
import jax.numpy as jnp
import numpy as np
from jax import lax
from jax.experimental import pallas as pl
from jax.experimental.pallas import tpu as pltpu
from jax.sharding import Mesh, PartitionSpec as P

SHOTS = 128
WINDOW = 512
FREQS = 16
TIMES = 32
SLOTS = 8
OWNERS = 32
PART_SHOTS = 16
SHOT_AXES = ("xl", "z", "core")
FREQ_AXES = ("xh", "y")
BF = jnp.bfloat16
F32 = jnp.float32


def transform_tables():
    f = np.arange(FREQS)[None, :]
    t = np.arange(TIMES)[:, None]
    angle = ((f + 1) * t) % (2 * FREQS) * (np.pi / FREQS)
    table = np.stack([np.cos(angle), -np.sin(angle)], axis=2) / FREQS
    table = table.reshape(TIMES, 2 * FREQS)
    eye = np.eye(PART_SHOTS)
    full = np.einsum("tq,ab->atqb", table, eye)
    full = full.reshape(PART_SHOTS * TIMES, 2 * FREQS * PART_SHOTS).astype(np.float32)
    high = full.astype(BF)
    low = (full - high.astype(np.float32)).astype(BF)
    order = np.einsum("ts,ab->tabs", np.eye(TIMES), eye)
    order = order.reshape(TIMES * PART_SHOTS, PART_SHOTS * TIMES).astype(BF)
    return high, low, order


def convolve_kernel(
    place, wave, a0p, a0q, a1p, a1q, a1w, g1, g1s, g2, g2s, out, acc_r, acc_i
):
    step = pl.program_id(0)
    xl = place[0]
    core = place[1]

    @pl.when(step == 0)
    def _():
        acc_r[...] = jnp.zeros_like(acc_r)
        acc_i[...] = jnp.zeros_like(acc_i)

    def rows(own, other, part):
        mine = own[0, part]
        theirs = other[0, part]
        first = jnp.where(core == 0, mine, theirs)
        second = jnp.where(core == 0, theirs, mine)
        return [first, second]

    def left(block, part, is_own_half):
        column = jnp.where(is_own_half, xl, 1 - xl) * 8 + step
        return jnp.where(column < 2, a1w[part], block[part])

    br = jnp.concatenate(rows(g1, g1s, 0) + rows(g2, g2s, 0), axis=0)
    bi = jnp.concatenate(rows(g1, g1s, 1) + rows(g2, g2s, 1), axis=0)
    ar = jnp.concatenate(
        [
            jnp.concatenate([a0p[0, 0], a0q[0, 0]], axis=1),
            jnp.concatenate([left(a1p, 0, True), left(a1q, 0, False)], axis=1),
        ],
        axis=0,
    )
    ai = jnp.concatenate(
        [
            jnp.concatenate([a0p[1, 0], a0q[1, 0]], axis=1),
            jnp.concatenate([left(a1p, 1, True), left(a1q, 1, False)], axis=1),
        ],
        axis=0,
    )
    dot = lambda a, b: jnp.dot(a, b, preferred_element_type=F32)
    acc_r[...] += dot(ar, br) - dot(ai, bi)
    acc_i[...] += dot(ar, bi) + dot(ai, br)

    @pl.when(step == pl.num_programs(0) - 1)
    def _():
        wr = wave[0, xl]
        wi = wave[1, xl]
        er = (acc_r[...] * wr - acc_i[...] * wi).astype(BF)
        ei = (acc_r[...] * wi + acc_i[...] * wr).astype(BF)
        for block in range(2):
            where = xl if block == 0 else 1 - xl
            for part in range(8):
                first = block * SHOTS + part * PART_SHOTS
                out[2 * part + where, 0:16, :] = er[first : first + 16]
                out[2 * part + where, 16:32, :] = ei[first : first + 16]


def convolve(place, wavelet, wavefield, swapped, swapped_window, g1, g1s, g2, g2s):
    a0 = lambda half: pl.BlockSpec(
        (2, 1, SHOTS, 256),
        lambda k, p: (0, p[0], 0, (p[0] if half == 0 else 1 - p[0]) * 8 + k),
    )
    a1 = lambda half: pl.BlockSpec(
        (2, SHOTS, 256),
        lambda k, p: (0, 0, jnp.maximum((p[0] if half == 0 else 1 - p[0]) * 8 + k - 2, 0)),
    )
    window = pl.BlockSpec((2, SHOTS, 256), lambda k, p: (0, 0, jnp.minimum(k, 1)))
    gathered = pl.BlockSpec((1, 2, SHOTS, WINDOW), lambda k, p: (k, 0, 0, 0))
    return pl.pallas_call(
        convolve_kernel,
        out_shape=jax.ShapeDtypeStruct((16, 32, WINDOW), BF),
        grid_spec=pltpu.PrefetchScalarGridSpec(
            num_scalar_prefetch=1,
            grid=(8,),
            in_specs=[pl.BlockSpec(memory_space=pltpu.SMEM)]
            + [a0(0), a0(1), a1(0), a1(1), window]
            + [gathered] * 4,
            out_specs=pl.BlockSpec((16, 32, WINDOW), lambda k, p: (0, 0, 0)),
            scratch_shapes=[pltpu.VMEM((256, WINDOW), F32)] * 2,
        ),
        compiler_params=pltpu.CompilerParams(
            dimension_semantics=("arbitrary",), vmem_limit_bytes=40 * 1024 * 1024
        ),
        cost_estimate=pl.CostEstimate(
            flops=2 * 256 * 4096 * 512 * 4, bytes_accessed=13 * 2**20, transcendentals=0
        ),
    )(place, wavelet, wavefield, wavefield, swapped, swapped, swapped_window, g1, g1s, g2, g2s)


def transform_kernel(spectra, high, low, order, trace_map, out, traces, moved):
    dot = lambda a, b: jnp.dot(a, b, preferred_element_type=F32)
    x = spectra[...].reshape(512, WINDOW)
    traces[...] = (dot(high[...], x) + dot(low[...], x)).astype(BF)
    receivers = lax.broadcasted_iota(jnp.int32, (WINDOW, WINDOW), 0)
    for shot in range(PART_SHOTS):
        chosen = jnp.where(receivers == trace_map[shot : shot + 1, :], 1.0, 0.0).astype(BF)
        picked = dot(traces[shot * TIMES : (shot + 1) * TIMES, :], chosen)
        moved[shot * TIMES : (shot + 1) * TIMES, :] = picked.astype(BF)
    out[...] = dot(order[...], moved[...]).astype(BF)


def transform(spectra, trace_map):
    high, low, order = transform_tables()
    return pl.pallas_call(
        transform_kernel,
        out_shape=jax.ShapeDtypeStruct((TIMES * PART_SHOTS, WINDOW), BF),
        scratch_shapes=[pltpu.VMEM((512, WINDOW), BF)] * 2,
        compiler_params=pltpu.CompilerParams(vmem_limit_bytes=40 * 1024 * 1024),
    )(spectra, jnp.asarray(high), jnp.asarray(low), jnp.asarray(order), trace_map)


def slot_matrix(owners):
    same = owners[:, None] == owners[None, :]
    position = jnp.arange(SHOTS, dtype=jnp.int32)
    rank = jnp.sum(same & (position[:, None] > position[None, :]), axis=1, dtype=jnp.int32)
    slot = owners * SLOTS + rank
    times = 4
    column = jnp.broadcast_to(slot.reshape(8, 1, PART_SHOTS), (8, times, PART_SHOTS))
    column_time = jnp.arange(times, dtype=jnp.int32)[None, :, None]
    key = ((column // SLOTS) * times + column_time) * SLOTS + column % SLOTS
    row = jnp.arange(OWNERS * times * SLOTS, dtype=jnp.int32)
    return (row[:, None] == key.reshape(1, 512)).astype(BF)


def shards(wavefield, wavelet, shot_owner, trace_map):
    xl = lax.axis_index("xl")
    core = lax.axis_index("core")
    group = lax.axis_index(FREQ_AXES)
    swap = [(0, 1), (1, 0)]
    own = lax.dynamic_slice_in_dim(wavefield[..., :WINDOW], xl, 1, 1)[:, 0]
    give_window = lax.dynamic_slice_in_dim(wavefield[..., :WINDOW], 1 - xl, 1, 1)[:, 0]
    give = lax.dynamic_slice_in_dim(wavefield[..., WINDOW:], 1 - xl, 1, 1)[:, 0]
    swapped_window = lax.ppermute(give_window, "xl", swap)
    g1 = lax.all_gather(own, "z", axis=0)
    swapped = lax.ppermute(give, "xl", swap)
    g2 = lax.all_gather(swapped_window, "z", axis=0)
    g1s = lax.ppermute(g1, "core", swap)
    g2s = lax.ppermute(g2, "core", swap)
    place = jnp.stack([xl, core]).astype(jnp.int32)
    estimate = convolve(
        place, wavelet, wavefield, swapped, swapped_window, g1, g1s, g2, g2s
    )
    spectra = lax.all_to_all(estimate, ("xh", "y", "xl"), 0, 0, tiled=True)
    part_map = lax.dynamic_slice_in_dim(trace_map, group * PART_SHOTS, PART_SHOTS, 0)
    arranged = transform(spectra, part_map)
    times = lax.all_to_all(arranged.reshape(8, 64, WINDOW), FREQ_AXES, 0, 0, tiled=True)
    slots = slot_matrix(shot_owner[:, 0])
    outgoing = jnp.dot(slots, times.reshape(512, WINDOW), preferred_element_type=F32)
    outgoing = outgoing.astype(BF).reshape(OWNERS, 4 * SLOTS, WINDOW)
    arrived = lax.all_to_all(outgoing, SHOT_AXES, 0, 0, tiled=True)
    arrived = arrived.reshape(OWNERS, 4, SLOTS, WINDOW)
    return jnp.transpose(arrived, (1, 0, 2, 3)).reshape(4, OWNERS * SLOTS, WINDOW)


def solution(mesh):
    fine = Mesh(mesh.devices.reshape(2, 8, 2, 2, 4), SHOT_AXES + FREQ_AXES)
    placed = (
        P(None, FREQ_AXES, SHOT_AXES, None),
        P(None, FREQ_AXES),
        P(SHOT_AXES, None),
        P(SHOT_AXES, None),
    )
    return jax.shard_map(
        shards,
        mesh=fine,
        in_specs=placed,
        out_specs=P(FREQ_AXES, SHOT_AXES, None),
        check_vma=False,
    )
```

time: 322 us -> 233 us (0.72)
  waiting for transfers between devices: 193 us -> 131 us
  matrix products: 45.3 us -> 0.72 us
  starting transfers between devices: 0.04 us -> 22.9 us
  Pallas kernels: 0 us -> 13.7 us
  local copies, waits for them, and re-layouts: 28.5 us -> 15.1 us
  loops' own time: 4.59 us -> 0 us
    reduce_scatter x1 -> x0, waiting for transfers between devices: 88.6 us -> none  [shards(): lax.psum_scatter((accumulated_sum - jnp.einsum('vq,qjl->vjl', odd_basis_t...]
    ppermute x0 -> x4, waiting for transfers between devices: none -> 45.3 us  [the longest x1 40.6 us: shards(): swapped = lax.ppermute(give, 'xl', swap)]
    dot_general x16 -> x1, matrix products: 45.3 us -> 0.72 us  [shards(): jnp.dot(slots, times.reshape(512, WINDOW), preferred_element_type=F32)]
    all_gather x1 -> x2, waiting for transfers between devices: 104 us -> 67.4 us  [the longest x1 37.1 us: shards(): g2 = lax.all_gather(swapped_window, 'z', axis=0)]
    all_to_all x0 -> x2, waiting for transfers between devices: none -> 18.5 us  [the longest x1 9.86 us: shards(): spectra = lax.all_to_all(estimate, ('xh', 'y', 'xl'), 0, 0, tiled=True)]
    dynamic_slice x24 -> x2, local copies, waits for them, and re-layouts: 17.6 us -> 0.77 us  [the longest x1 0.76 us: shards(): own = lax.dynamic_slice_in_dim(wavefield[..., :WINDOW], xl, 1, 1)[:, 0]]
    pallas_call x0 -> x2, Pallas kernels: none -> 13.7 us  [the longest x1 10.3 us: convolve(): pl.pallas_call(convolve_kernel, out_shape=jax.ShapeDtypeStruct((16, 32, W...]
    ppermute x0 -> x4, starting transfers between devices: none -> 12.1 us  [the longest x1 4.39 us: shards(): g1s = lax.ppermute(g1, 'core', swap)]
  transfers between devices with their start and end apart: 2 -> 8, of which waited for: 2 -> 6; matrix products, arithmetic and copies ran while one was open for 0% -> 3% of each run, Pallas kernels for 0% -> 0%
where the time goes in v1:
time: 233 us; the launch traced here: 231 us
  waiting for transfers between devices  131 us (56%)
  blocking collectives  34 us (15%)
  starting transfers between devices  22.9 us (10%)
  local copies, waits for them, and re-layouts  15.1 us (6%)
  Pallas kernels  13.7 us (6%)
  between operations  13.5 us (6%)
    ppermute x1, waiting for transfers between devices, shards(): swapped = lax.ppermute(give, 'xl', swap)  40.6 us
    all_gather x1, waiting for transfers between devices, shards(): g2 = lax.all_gather(swapped_window, 'z', axis=0)  37.1 us
    all_to_all x1, blocking collectives, shards(): arrived = lax.all_to_all(outgoing, SHOT_AXES, 0, 0, tiled=True)  34 us
    all_gather x1, waiting for transfers between devices, shards(): g1 = lax.all_gather(own, 'z', axis=0)  30.3 us
    pallas_call x1, Pallas kernels, convolve(): pl.pallas_call(convolve_kernel, out_shape=jax.ShapeDtypeStruct((16, 32, W...  10.3 us
    all_to_all x1, waiting for transfers between devices, shards(): spectra = lax.all_to_all(estimate, ('xh', 'y', 'xl'), 0, 0, tiled=True)  9.86 us
    all_to_all x1, waiting for transfers between devices, shards(): lax.all_to_all(arranged.reshape(8, 64, WINDOW), FREQ_AXES, 0, 0, tiled=True)  8.59 us
    all_to_all x1, starting transfers between devices, shards(): spectra = lax.all_to_all(estimate, ('xh', 'y', 'xl'), 0, 0, tiled=True)  6.53 us
  transfers between devices with their start and end apart: 8, of which 6 were waited for; matrix products, arithmetic and copies ran while one was open for 3% of the time, Pallas kernels for 0%

profile of v1, /device:TPU:1, one launch (start us, length us, event | category | flops | bytes accessed | tf_op | source)
XLA Modules:
  0.0 231.4 jit_solution(12613920049475600266)
XLA Ops:
  6.5 1.1 slice.8
  7.7 0.8 constant_dynamic-slice_fusion.1
  8.4 0.0 all-gather.5.cloned.1.call-update
  8.4 0.0 all-gather.7.cloned.1.call-start
  8.5 2.1 collective-permute-start.1
  10.6 4.7 %collective-permute-done.1.a1w = bf16[2,128,512]{2,1,0:T(8,128)(2,1)S(1)} collective-permute-done((bf16[2,128,512]{2,1,0:T(8,128)(2,1)S(1)}, bf16[2,128,512]{2,1,0:T(8,128)(2,1)S(1)}, u32[]{:S(2)}, u32[]{:S(2)}) %collective-permute-start.1) | collective-permute-done | bytes 262176 | tf_op jit(solution)/shard_map/ppermute | solution.py:170
  15.3 0.7 copy-done.3
  16.0 4.1 %slice.7 = bf16[2,2,128,3584]{3,2,1,0:T(8,128)(2,1)} slice(bf16[2,2,128,4096]{3,2,1,0:T(8,128)(2,1)} %a0q.1), slice={[0:2], [0:2], [0:128], [512:4096]} | slice | bytes 7340032 | tf_op jit(solution)/shard_map/slice | solution.py:169
  20.1 30.3 %all-gather.5.cloned.1.call-done = bf16[16,1,128,512]{3,2,1,0:T(8,128)(2,1)} async-done(((bf16[2,1,128,512]{3,2,1,0:T(8,128)(2,1)}), bf16[16,1,128,512]{3,2,1,0:T(8,128)(2,1)}) %all-gather.5.cloned.1.call-update) | async-done | bytes 2097168 | tf_op jit(solution)/shard_map/all_gather | solution.py:171
  50.4 4.4 %collective-permute-start.2 = (bf16[8,2,128,512]{3,2,1,0:T(8,128)(2,1)}, bf16[8,2,128,512]{3,2,1,0:T(8,128)(2,1)}, u32[]{:S(2)}, u32[]{:S(2)}) collective-permute-start(bf16[8,2,128,512]{3,2,1,0:T(8,128)(2,1)} %bitcast.20), channel_id=1, source_target_pairs={{0,8},{8,0},{1,9},{9,1},{2,10},{10,2},{3,11},{11,3},{4,12},{12,4},... | collective-permute-start | bytes 6291464 | tf_op jit(solution)/shard_map/ppermute | solution.py:174
  54.8 37.1 %all-gather.7.cloned.1.call-done = bf16[16,128,512]{2,1,0:T(8,128)(2,1)} async-done(((bf16[2,128,512]{2,1,0:T(8,128)(2,1)}), bf16[16,128,512]{2,1,0:T(8,128)(2,1)}) %all-gather.7.cloned.1.call-update) | async-done | bytes 2097168 | tf_op jit(solution)/shard_map/all_gather | solution.py:173
  91.9 4.4 %collective-permute-start.3 = (bf16[8,2,128,512]{3,2,1,0:T(8,128)(2,1)}, bf16[8,2,128,512]{3,2,1,0:T(8,128)(2,1)}, u32[]{:S(2)}, u32[]{:S(2)}) collective-permute-start(bf16[8,2,128,512]{3,2,1,0:T(8,128)(2,1)} %bitcast.22), channel_id=1, source_target_pairs={{0,8},{8,0},{1,9},{9,1},{2,10},{10,2},{3,11},{11,3},{4,12},{12,4},... | collective-permute-start | bytes 6291464 | tf_op jit(solution)/shard_map/ppermute | solution.py:175
  96.2 2.9 %dynamic-slice_bitcast_fusion = bf16[2,128,3584]{2,1,0:T(8,128)(2,1)} fusion(bf16[2,2,128,3584]{3,2,1,0:T(8,128)(2,1)} %slice.7, s32[]{:T(128)S(6)} %select_n.37), kind=kLoop, calls=%fused_computation.2 | loop fusion | bytes 3670020 | tf_op jit(solution)/shard_map/squeeze | solution.py:169
  99.2 1.2 collective-permute-start
  100.4 0.1 pad_add_fusion.place
  100.4 40.6 %collective-permute-done.a1p.a1q = bf16[2,128,3584]{2,1,0:T(8,128)(2,1)S(1)} collective-permute-done((bf16[2,128,3584]{2,1,0:T(8,128)(2,1)}, bf16[2,128,3584]{2,1,0:T(8,128)(2,1)S(1)}, u32[]{:S(2)}, u32[]{:S(2)}) %collective-permute-start) | collective-permute-done | bytes 1835040 | tf_op jit(solution)/shard_map/ppermute | solution.py:172
  141.1 1.6 copy-done.1
  142.6 1.6 copy-done.2
  144.2 10.3 %shard_map.73 = bf16[16,32,512]{2,1,0:T(8,128)(2,1)} custom-call(s32[2]{0:T(128)S(1)} %pad_add_fusion.place, f32[2,2]{1,0:T(2,128)S(1)} %copy-done.8, bf16[2,2,128,4096]{3,2,1,0:T(8,128)(2,1)} %a0q.1, bf16[2,2,128,4096]{3,2,1,0:T(8,128)(2,1)} %a0q.1, bf16[2,128,3584]{2,1,0:T(8,128)(2,1)S(1)} %collective-permute-done.a1p.a1q, ...), custom_call_target="tpu_custom_call" | custom-call | flops 4294967296 | bytes 13631488 | tf_op jit(solution)/shard_map/pallas_call | solution.py:106
  154.6 6.5 %all-to-all-start = ((bf16[16,32,512]{2,1,0:T(8,128)(2,1)}), bf16[16,32,512]{2,1,0:T(8,128)(2,1)S(1)}, u32[]{:S(2)}, u32[]{:S(2)}) async-start(bf16[16,32,512]{2,1,0:T(8,128)(2,1)} %shard_map.73), calls=%async_computation | async-start | bytes 1048576 | tf_op jit(solution)/shard_map/all_to_all | solution.py:180
  161.1 0.1 mul.44
  161.2 0.2 convert_reduce_fusion
  161.4 0.1 reduce_sum.12
  161.5 9.9 %all-to-all-done.spectra = bf16[16,32,512]{2,1,0:T(8,128)(2,1)S(1)} async-done(((bf16[16,32,512]{2,1,0:T(8,128)(2,1)}), bf16[16,32,512]{2,1,0:T(8,128)(2,1)S(1)}, u32[]{:S(2)}, u32[]{:S(2)}) %all-to-all-start) | async-done | bytes 524320 | tf_op jit(solution)/shard_map/all_to_all | solution.py:180
  171.4 1.0 copy-done.7
  172.4 3.3 %shard_map.74 = bf16[512,512]{1,0:T(8,128)(2,1)} custom-call(bf16[16,32,512]{2,1,0:T(8,128)(2,1)S(1)} %all-to-all-done.spectra, bf16[512,512]{1,0:T(8,128)(2,1)S(1)} %copy-done.5, bf16[512,512]{1,0:T(8,128)(2,1)S(1)} %copy-done.6, bf16[512,512]{1,0:T(8,128)(2,1)S(1)} %copy-done.7, s32[16,512]{1,0:T(8,128)S(1)} %constant_dynamic-slice_fusion.trace_map), custom_call_target="tpu_custom_call" | custom-call | tf_op jit(solution)/shard_map/pallas_call | solution.py:141
  175.7 4.3 %all-to-all-start.1 = ((bf16[8,64,512]{2,1,0:T(8,128)(2,1)}), bf16[8,64,512]{2,1,0:T(8,128)(2,1)S(1)}, u32[]{:S(2)}, u32[]{:S(2)}) async-start(bf16[8,64,512]{2,1,0:T(8,128)(2,1)} %bitcast.7), calls=%async_computation.1 | async-start | bytes 1048576 | tf_op jit(solution)/shard_map/all_to_all | solution.py:183
  180.1 0.1 reshape.109
  180.2 8.6 %all-to-all-done.1 = bf16[8,64,512]{2,1,0:T(8,128)(2,1)S(1)} async-done(((bf16[8,64,512]{2,1,0:T(8,128)(2,1)}), bf16[8,64,512]{2,1,0:T(8,128)(2,1)S(1)}, u32[]{:S(2)}, u32[]{:S(2)}) %all-to-all-start.1) | async-done | bytes 524320 | tf_op jit(solution)/shard_map/all_to_all | solution.py:183
  188.7 0.7 fusion.1
  189.5 34.0 %all_to_all.15 = bf16[32,32,512]{2,1,0:T(8,128)(2,1)S(1)} all-to-all(bf16[32,32,512]{2,1,0:T(8,128)(2,1)S(1)} %bitcast.24), channel_id=1, replica_groups=mesh['xl'=2,'z'=8,'core'=2,'xh'=2,'y'=4] {'xl','z','core'}, dimensions={0} | all-to-all | bytes 2097152 | tf_op jit(solution)/shard_map/all_to_all | solution.py:187
  223.5 1.1 copy_bitcast_fusion
  (26 shorter events, 0.1 us)
Async XLA Ops:
  6.5 154.9 %copy-start = (s32[128,512]{1,0:T(8,128)S(1)}, s32[128,512]{1,0:T(8,128)}, u32[]{:S(2)}) copy-start(s32[128,512]{1,0:T(8,128)} %param.10) | copy-start | bytes 786436
  6.5 43.8 %all-gather.5.cloned.1.call-start = ((), (), s32[]{:S(2)}) async-start(), calls=%async_computation.3 | async-start | bytes 2359296 | tf_op jit(solution)/shard_map/all_gather | solution.py:171
  8.4 83.4 %all-gather.7.cloned.1.call-start = ((), (), s32[]{:S(2)}) async-start(), calls=%async_computation.4 | async-start | bytes 2359296 | tf_op jit(solution)/shard_map/all_gather | solution.py:173
  8.5 6.8 %collective-permute-start.1 = (bf16[2,128,512]{2,1,0:T(8,128)(2,1)S(1)}, bf16[2,128,512]{2,1,0:T(8,128)(2,1)S(1)}, u32[]{:S(2)}, u32[]{:S(2)}) collective-permute-start(bf16[2,128,512]{2,1,0:T(8,128)(2,1)S(1)} %get-tuple-element.10), channel_id=1, source_target_pairs={{0,128},{128,0},{1,129},{129,1},{2,130},{130,2},{3,131},{131,3},{4... | collective-permute-start | bytes 786440 | tf_op jit(solution)/shard_map/ppermute | solution.py:170
  15.3 0.7 copy-start.3
  20.1 120.9 %copy-start.4 = (bf16[2,128,512]{2,1,0:T(8,128)(2,1)S(1)}, bf16[2,128,512]{2,1,0:T(8,128)(2,1)}, u32[]{:S(2)}) copy-start(bf16[2,128,512]{2,1,0:T(8,128)(2,1)} %copy-done.3) | copy-start | bytes 786436
  20.1 121.0 %copy-start.8 = (f32[2,2]{1,0:T(2,128)S(1)}, f32[2,2]{1,0:T(2,128)}, u32[]{:S(2)}) copy-start(f32[2,2]{1,0:T(2,128)} %wave.1) | copy-start | bytes 52
  50.4 90.6 %collective-permute-start.2 = (bf16[8,2,128,512]{3,2,1,0:T(8,128)(2,1)}, bf16[8,2,128,512]{3,2,1,0:T(8,128)(2,1)}, u32[]{:S(2)}, u32[]{:S(2)}) collective-permute-start(bf16[8,2,128,512]{3,2,1,0:T(8,128)(2,1)} %bitcast.20), channel_id=1, source_target_pairs={{0,8},{8,0},{1,9},{9,1},{2,10},{10,2},{3,11},{11,3},{4,12},{12,4},... | collective-permute-start | bytes 6291464 | tf_op jit(solution)/shard_map/ppermute | solution.py:174
  91.9 49.2 %collective-permute-start.3 = (bf16[8,2,128,512]{3,2,1,0:T(8,128)(2,1)}, bf16[8,2,128,512]{3,2,1,0:T(8,128)(2,1)}, u32[]{:S(2)}, u32[]{:S(2)}) collective-permute-start(bf16[8,2,128,512]{3,2,1,0:T(8,128)(2,1)} %bitcast.22), channel_id=1, source_target_pairs={{0,8},{8,0},{1,9},{9,1},{2,10},{10,2},{3,11},{11,3},{4,12},{12,4},... | collective-permute-start | bytes 6291464 | tf_op jit(solution)/shard_map/ppermute | solution.py:175
  99.2 41.9 %collective-permute-start = (bf16[2,128,3584]{2,1,0:T(8,128)(2,1)}, bf16[2,128,3584]{2,1,0:T(8,128)(2,1)S(1)}, u32[]{:S(2)}, u32[]{:S(2)}) collective-permute-start(bf16[2,128,3584]{2,1,0:T(8,128)(2,1)} %dynamic-slice_bitcast_fusion), channel_id=1, source_target_pairs={{0,128},{128,0},{1,129},{129,1},{2,130},{130,2},{3,131},{131,3},{4... | collective-permute-start | bytes 5505032 | tf_op jit(solution)/shard_map/ppermute | solution.py:172
  100.4 60.8 %copy-start.9 = (s32[128,1]{0,1:T(1,128)S(1)}, s32[128,1]{0,1:T(1,128)}, u32[]{:S(2)}) copy-start(s32[128,1]{0,1:T(1,128)} %param.9) | copy-start | bytes 1540
  141.0 1.6 copy-start.1
  142.6 1.6 copy-start.2
  144.2 27.2 %copy-start.5 = (bf16[512,512]{1,0:T(8,128)(2,1)S(1)}, bf16[512,512]{1,0:T(8,128)(2,1)}, u32[]{:S(2)}) copy-start(bf16[512,512]{1,0:T(8,128)(2,1)} %constant.66.clone.high) | copy-start | bytes 1572868
  144.2 27.2 %copy-start.6 = (bf16[512,512]{1,0:T(8,128)(2,1)S(1)}, bf16[512,512]{1,0:T(8,128)(2,1)}, u32[]{:S(2)}) copy-start(bf16[512,512]{1,0:T(8,128)(2,1)} %constant.67.clone.low) | copy-start | bytes 1572868
  154.6 16.8 %all-to-all-start = ((bf16[16,32,512]{2,1,0:T(8,128)(2,1)}), bf16[16,32,512]{2,1,0:T(8,128)(2,1)S(1)}, u32[]{:S(2)}, u32[]{:S(2)}) async-start(bf16[16,32,512]{2,1,0:T(8,128)(2,1)} %shard_map.73), calls=%async_computation | async-start | bytes 1048576 | tf_op jit(solution)/shard_map/all_to_all | solution.py:180
  171.4 1.0 copy-start.7
  175.7 13.0 %all-to-all-start.1 = ((bf16[8,64,512]{2,1,0:T(8,128)(2,1)}), bf16[8,64,512]{2,1,0:T(8,128)(2,1)S(1)}, u32[]{:S(2)}, u32[]{:S(2)}) async-start(bf16[8,64,512]{2,1,0:T(8,128)(2,1)} %bitcast.7), calls=%async_computation.1 | async-start | bytes 1048576 | tf_op jit(solution)/shard_map/all_to_all | solution.py:183
Sparse Core Ops, SparseCore 0:
  9.1 41.1 all-gather.4
  52.2 39.6 all-gather.6

commit v2 on v1

v2 whole, which is shorter than its diff:
```python
import jax
import jax.numpy as jnp
import numpy as np
from jax import lax
from jax.experimental import pallas as pl
from jax.experimental.pallas import tpu as pltpu
from jax.sharding import Mesh, PartitionSpec as P

SHOTS = 128
WINDOW = 512
FREQS = 16
TIMES = 32
OWNERS = 32
PART_SHOTS = 16
DEPTH = 8
SHOT_AXES = ("xl", "z", "core")
FREQ_AXES = ("xh", "y")
BF = jnp.bfloat16
F32 = jnp.float32
PARAMS = pltpu.CompilerParams(vmem_limit_bytes=48 * 1024 * 1024)


def dot(a, b):
    return jnp.dot(a, b, preferred_element_type=F32)


def transform_tables():
    f = np.arange(FREQS)[None, :]
    t = np.arange(TIMES)[:, None]
    angle = ((f + 1) * t) % (2 * FREQS) * (np.pi / FREQS)
    table = np.stack([np.cos(angle), -np.sin(angle)], axis=2) / FREQS
    table = table.reshape(TIMES, 2 * FREQS)
    full = np.einsum("tq,ab->atqb", table, np.eye(PART_SHOTS))
    full = full.reshape(PART_SHOTS * TIMES, 2 * FREQS * PART_SHOTS).astype(np.float32)
    high = full.astype(BF)
    low = (full - high.astype(np.float32)).astype(BF)
    return high, low


HBM = pl.BlockSpec(memory_space=pltpu.HBM)
ANY = pl.BlockSpec(memory_space=pl.ANY)
SMEM = pl.BlockSpec(memory_space=pltpu.SMEM)
CHUNK = 1024
STRIP = 16


def run_copies(pairs, sems):
    copies = [
        pltpu.make_async_copy(source, target, sems.at[n])
        for n, (source, target) in enumerate(pairs)
    ]
    for copy in copies:
        copy.start()
    return copies


def window_kernel(place, wave, strip, own, give, sems):
    pairs = []
    for target, freq in ((own, place[0]), (give, 1 - place[0])):
        for part in range(2):
            for column in range(4):
                pairs.append(
                    (
                        wave.at[part, freq, :, pl.ds(column * 128, 128)],
                        target.at[pl.ds((part * 4 + column) * 128, 128), :],
                    )
                )
        pairs.append((strip, target.at[pl.ds(CHUNK, STRIP), :]))
    for copy in run_copies(pairs, sems):
        copy.wait()


def window_chunks(place, wavefield, strip):
    return pl.pallas_call(
        window_kernel,
        out_shape=[jax.ShapeDtypeStruct((CHUNK + STRIP, 128), BF)] * 2,
        in_specs=[SMEM, HBM, ANY],
        out_specs=[ANY] * 2,
        scratch_shapes=[pltpu.SemaphoreType.DMA((18,))],
        compiler_params=PARAMS,
    )(place, wavefield, strip)


def halves_kernel(place, wave, diag, same, partner, far, near, sems):
    xl, core = place[0], place[1]
    copies = run_copies(
        [
            (wave.at[0, 1 - xl, :, pl.ds(WINDOW, 3584)], far.at[0]),
            (wave.at[1, 1 - xl, :, pl.ds(WINDOW, 3584)], far.at[1]),
            (wave.at[0, xl], near.at[0]),
            (wave.at[1, xl], near.at[1]),
        ],
        sems,
    )
    for n, copy in enumerate(copies):
        copy.wait()
        part = n % 2
        here = far if n < 2 else near
        for block in range(14 if n < 2 else 16):
            a = here[part, :, block * 256 : block * 256 + 128]
            b = here[part, :, block * 256 + 128 : block * 256 + 256]
            target = slice(block * 128, block * 128 + 128)
            if n < 2:
                same[part, :, target] = jnp.where(core == 0, a, b)
                diag[part, :, target] = jnp.where(core == 0, b, a)
            else:
                partner[part, :, target] = jnp.where(core == 0, b, a)


def column_halves(place, wavefield):
    return pl.pallas_call(
        halves_kernel,
        out_shape=[
            jax.ShapeDtypeStruct((2, SHOTS, 1792), BF),
            jax.ShapeDtypeStruct((2, SHOTS, 1792), BF),
            jax.ShapeDtypeStruct((2, SHOTS, 2048), BF),
        ],
        in_specs=[SMEM, HBM],
        scratch_shapes=[
            pltpu.VMEM((2, SHOTS, 3584), BF),
            pltpu.VMEM((2, SHOTS, 4096), BF),
            pltpu.SemaphoreType.DMA((4,)),
        ],
        compiler_params=PARAMS,
    )(place, wavefield)


def follow_kernel(value, earlier, out):
    pass


def follow(value, earlier, flops=0):
    return pl.pallas_call(
        follow_kernel,
        cost_estimate=pl.CostEstimate(flops=flops, bytes_accessed=flops // 500, transcendentals=0),
        out_shape=jax.ShapeDtypeStruct(value.shape, value.dtype),
        in_specs=[pl.BlockSpec(memory_space=pl.ANY)] * 2,
        out_specs=pl.BlockSpec(memory_space=pl.ANY),
        input_output_aliases={0: 0},
    )(value, earlier)


def pick(place, block, refs, part):
    if len(refs) == 1:
        return refs[0][part, :, pl.ds(pl.multiple_of(block * 128, 128), 128)]
    rest, window = refs
    late = jnp.maximum(block - 2, 0)
    early = jnp.minimum(block, 1) * 2 + place[1]
    a = rest[part, :, pl.ds(pl.multiple_of(late * 128, 128), 128)]
    b = window[pl.ds(pl.multiple_of((part * 4 + early) * 128, 128), 128), :]
    return jnp.where(block < 2, b, a)


def window_columns(chunk, part):
    return jnp.concatenate(
        [chunk[(part * 4 + n) * 128 : (part * 4 + n + 1) * 128, :] for n in range(4)], axis=1
    )


def multiply(place, rows, near, far, depth):
    xl = place[0]
    sides = []
    for part in range(2):
        lines = []
        for refs in rows:
            a = pick(place, xl * DEPTH + depth, refs, part)
            b = pick(place, (1 - xl) * DEPTH + depth, refs, part)
            lines.append(jnp.concatenate([a, b], axis=1))
        sides.append(jnp.concatenate(lines, axis=0))
    ar, ai = sides
    lines = jnp.concatenate([ar, -ai], axis=1), jnp.concatenate([ai, ar], axis=1)
    columns = [window_columns(chunk, part) for part in range(2) for chunk in (near, far)]
    return dot(jnp.concatenate(lines, axis=0), jnp.concatenate(columns, axis=0))


def product(place, wavefield, line, other_line, near, far):
    distances = list(far)
    count = len(distances)
    size = 2 * SHOTS
    rest, window = other_line

    def kernel(place, line_in, rest_in, window_in, *refs):
        near_in, far_in = refs[:count], refs[count : 2 * count]
        out, total, near_here, far_here, line_here, rest_here, window_here, sems = refs[2 * count :]
        pairs = [(rest_in, rest_here), (window_in.at[pl.ds(0, CHUNK), :], window_here)]
        if line is None:
            for block in range(16):
                column = pl.multiple_of((2 * block + place[1]) * 128, 128)
                pairs.append(
                    (
                        line_in.at[:, place[0], :, pl.ds(column, 128)],
                        line_here.at[:, :, pl.ds(block * 128, 128)],
                    )
                )
        else:
            pairs.append((line_in, line_here))
        first = len(pairs)
        for n in range(count):
            pairs.append((near_in[n].at[pl.ds(0, CHUNK), :], near_here.at[n]))
            pairs.append((far_in[n].at[pl.ds(0, CHUNK), :], far_here.at[n]))
        copies = run_copies(pairs, sems)
        for copy in copies[:first]:
            copy.wait()
        groups = [(line_here,), (rest_here, window_here)]
        for n in range(count):
            copies[first + 2 * n].wait()
            copies[first + 2 * n + 1].wait()
            depth = lax.rem(place[2] - distances[n] + 2 * DEPTH, DEPTH)
            value = multiply(place, groups, near_here.at[n], far_here.at[n], depth)
            if n == 0:
                total[...] = value
            elif n < count - 1:
                total[...] += value
            else:
                out[0] = total[:size] + value[:size]
                out[1] = total[size:] + value[size:]

    return pl.pallas_call(
        kernel,
        out_shape=jax.ShapeDtypeStruct((2, size, WINDOW), F32),
        in_specs=[SMEM, HBM if line is None else ANY] + [ANY] * (2 + 2 * count),
        scratch_shapes=[
            pltpu.VMEM((2 * size, WINDOW), F32),
            pltpu.VMEM((count, CHUNK, 128), BF),
            pltpu.VMEM((count, CHUNK, 128), BF),
            pltpu.VMEM((2, SHOTS, 2048), BF),
            pltpu.VMEM(rest.shape, BF),
            pltpu.VMEM((CHUNK, 128), BF),
            pltpu.SemaphoreType.DMA((18 + 2 * count,)),
        ],
        compiler_params=PARAMS,
        cost_estimate=pl.CostEstimate(
            flops=2 * size * 512 * 1024 * count, bytes_accessed=2**22, transcendentals=0
        ),
    )(
        place,
        wavefield if line is None else line,
        rest,
        window,
        *[near[d] for d in distances],
        *[far[d] for d in distances],
    )


def scale_kernel(place, wave, keep, came, order_own, order_other, out):
    xl = place[0]
    wr = wave[0, xl]
    wi = wave[1, xl]
    for block in range(2):
        where = xl if block == 0 else 1 - xl
        order = order_own[...] if block == 0 else order_other[...]
        rows = slice(block * SHOTS, (block + 1) * SHOTS)
        real = keep[0, rows] + came[0, rows]
        imag = keep[1, rows] + came[1, rows]
        er = (real * wr - imag * wi).astype(BF)
        ei = (real * wi + imag * wr).astype(BF)
        sr = dot(order, er).astype(BF)
        si = dot(order, ei).astype(BF)
        for part in range(8):
            some = slice(part * PART_SHOTS, (part + 1) * PART_SHOTS)
            out[2 * part + where, 0:16, :] = sr[some]
            out[2 * part + where, 16:32, :] = si[some]


def scale(place, wavelet, keep, came, order_own, order_other):
    return pl.pallas_call(
        scale_kernel,
        out_shape=jax.ShapeDtypeStruct((16, 32, WINDOW), BF),
        in_specs=[pl.BlockSpec(memory_space=pltpu.SMEM)] * 2
        + [pl.BlockSpec(memory_space=pltpu.VMEM)] * 4,
        compiler_params=PARAMS,
    )(place, wavelet, keep, came, order_own, order_other)


def transform_kernel(spectra, high, low, trace_map, spread, swapped, out, traces, moved):
    x = spectra[...].reshape(512, WINDOW)
    traces[...] = (dot(high[...], x) + dot(low[...], x)).astype(BF)
    receivers = lax.broadcasted_iota(jnp.int32, (WINDOW, WINDOW), 0)
    for shot in range(PART_SHOTS):
        rows = slice(shot * TIMES, (shot + 1) * TIMES)
        chosen = jnp.where(receivers == trace_map[shot : shot + 1, :], 1.0, 0.0).astype(BF)
        moved[rows, :] = dot(traces[rows, :], chosen).astype(BF)
    upper = lax.broadcasted_iota(jnp.int32, (128, 8, 128), 1) < 4
    even, odd = [], []
    for pair in range(2):
        first = slice(pair * 256, pair * 256 + 128)
        second = slice(pair * 256 + 128, pair * 256 + 256)
        both = moved[:, pair * 256 : (pair + 1) * 256]
        plain = dot(spread[...], both).reshape(128, 8, 256)
        other = dot(swapped[...], both).reshape(128, 8, 256)
        even.append(jnp.where(upper, plain[..., :128], other[..., 128:]))
        odd.append(jnp.where(upper, other[..., :128], plain[..., 128:]))
    out[:, 0] = jnp.concatenate(even, axis=1).astype(BF)
    out[:, 1] = jnp.concatenate(odd, axis=1).astype(BF)


def transform(spectra, trace_map, spread, swapped):
    high, low = transform_tables()
    return pl.pallas_call(
        transform_kernel,
        out_shape=jax.ShapeDtypeStruct((128, 2, 16, 128), BF),
        scratch_shapes=[pltpu.VMEM((512, WINDOW), BF)] * 2,
        compiler_params=PARAMS,
    )(spectra, jnp.asarray(high), jnp.asarray(low), trace_map, spread, swapped)


def place_kernel(arrived, turns, out):
    for pair in range(16):
        block = arrived[pair * 16 : (pair + 1) * 16].reshape(256, 128)
        turned = dot(turns[pair], block).astype(BF)
        for column in range(4):
            for time in range(4):
                first = (column * 4 + time) * 16
                out[time, pair * 16 : (pair + 1) * 16, column * 128 : (column + 1) * 128] = (
                    turned[first : first + 16]
                )


def place_rows(arrived, turns):
    return pl.pallas_call(
        place_kernel,
        out_shape=jax.ShapeDtypeStruct((4, OWNERS * 8, WINDOW), BF),
        compiler_params=PARAMS,
    )(arrived, turns)


def sorted_positions(owners):
    shot = jnp.arange(SHOTS, dtype=jnp.int32)
    less = owners[None, :] < owners[:, None]
    same = (owners[None, :] == owners[:, None]) & (shot[None, :] < shot[:, None])
    return jnp.sum((less | same).astype(jnp.int32), axis=1)


def deal_order(position):
    row = jnp.arange(SHOTS, dtype=jnp.int32)
    wanted = (row % PART_SHOTS) * 8 + row // PART_SHOTS
    return (wanted[:, None] == position[None, :]).astype(BF)


def turn_matrices(near_owners, sources, me):
    number = jnp.arange(OWNERS, dtype=jnp.int32)
    before = jnp.sum((near_owners < me).astype(jnp.int32), axis=1)
    start = jnp.sum(
        jnp.where(number[:, None] == sources[None, :], before[None, :], 0), axis=1
    )
    group = jnp.arange(8, dtype=jnp.int32)
    rank = (group[None, :] - start[:, None] + SHOTS) % 8
    rank = rank.reshape(16, 2, 8, 1, 1)
    source = jnp.arange(2, dtype=jnp.int32).reshape(1, 2, 1, 1, 1)
    column = jnp.arange(4, dtype=jnp.int32).reshape(1, 1, 1, 4, 1)
    time = jnp.arange(4, dtype=jnp.int32).reshape(1, 1, 1, 1, 4)
    key = (column * 64 + time * 16 + source * 8 + rank).reshape(16, 1, 256)
    return (jnp.arange(256, dtype=jnp.int32)[None, :, None] == key).astype(BF)


def shards(wavefield, wavelet, shot_owner, trace_map):
    xl = lax.axis_index("xl")
    core = lax.axis_index("core")
    depth = lax.axis_index("z")
    group = lax.axis_index(FREQ_AXES)
    me = lax.axis_index(SHOT_AXES)
    swap = [(0, 1), (1, 0)]
    cross = [(n, 3 - n) for n in range(4)]
    right = [(n, (n + 1) % DEPTH) for n in range(DEPTH)]
    left = [(n, (n - 1) % DEPTH) for n in range(DEPTH)]
    place = jnp.stack([xl, core, depth]).astype(jnp.int32)

    owners = shot_owner[:, 0]
    strip = jnp.broadcast_to(owners.astype(BF)[None], (STRIP, SHOTS))
    own_window, give_window = window_chunks(place, wavefield, strip)
    xw = lax.ppermute(give_window, "xl", swap)
    diag, same, partner = column_halves(place, wavefield)
    diag = lax.ppermute(diag, ("xl", "core"), cross)
    partner = lax.ppermute(partner, "core", swap)
    same = lax.ppermute(follow(same, diag, 3 * 10**10), "xl", swap)
    xpw = lax.ppermute(xw, "core", swap)
    near = {0: own_window}
    far = {0: xw}
    for step in range(1, 5):
        near[step] = lax.ppermute(near[step - 1], "z", right)
        far[-step] = lax.ppermute(far[1 - step], "z", left)
        if step < 4:
            near[-step] = lax.ppermute(near[1 - step], "z", left)
            far[step] = lax.ppermute(far[step - 1], "z", right)
    far[4] = far.pop(-4)
    send = product(place, wavefield, partner, (diag, xpw), near, far)
    came = lax.ppermute(send, "core", swap)
    keep = product(place, wavefield, None, (same, xw), near, far)

    other_owners = xw[CHUNK].astype(jnp.int32)
    distances = list(far)
    strips = [near[d][CHUNK : CHUNK + 1] for d in distances]
    strips += [far[d][CHUNK : CHUNK + 1] for d in distances]
    strips = jnp.concatenate(strips, axis=0)
    near_owners = jnp.concatenate([strips, lax.ppermute(strips, "core", swap)], axis=0)
    near_owners = near_owners.astype(jnp.int32)
    depths = (depth - jnp.asarray(distances, dtype=jnp.int32) + DEPTH) % DEPTH * 2
    sources = jnp.concatenate([depths + 16 * xl, depths + 16 * (1 - xl)])
    sources = jnp.concatenate([sources + core, sources + 1 - core])
    position = sorted_positions(owners)
    order_own = deal_order(position)
    order_other = deal_order(sorted_positions(other_owners))
    wanted = jnp.arange(PART_SHOTS, dtype=jnp.int32) * 8 + group
    mine = wanted[:, None] == position[None, :]
    part_map = jnp.sum(jnp.where(mine[:, :, None], trace_map[None], 0), axis=1)
    part_owner = jnp.sum(jnp.where(mine, owners[None, :], 0), axis=1)
    key = part_owner[:, None] * TIMES + jnp.arange(TIMES, dtype=jnp.int32)[None, :]
    key = key.reshape(1, PART_SHOTS * TIMES)
    line = jnp.arange(OWNERS * TIMES, dtype=jnp.int32)[:, None]
    spread = (line == key).astype(BF)
    swapped = (line == key + 4 - 8 * ((key // 4) % 2)).astype(BF)

    estimate = scale(place, wavelet, keep, came, order_own, order_other)
    spectra = lax.all_to_all(estimate, FREQ_AXES + ("xl",), 0, 0, tiled=True)
    turns = turn_matrices(near_owners, sources, me)
    rows = transform(spectra, part_map, spread, swapped).reshape(256, 16, 128)
    arrived = lax.all_to_all(rows, SHOT_AXES + FREQ_AXES, 0, 0, tiled=True)
    return place_rows(arrived, turns)


def solution(mesh):
    fine = Mesh(mesh.devices.reshape(2, 8, 2, 2, 4), SHOT_AXES + FREQ_AXES)
    placed = (
        P(None, FREQ_AXES, SHOT_AXES, None),
        P(None, FREQ_AXES),
        P(SHOT_AXES, None),
        P(SHOT_AXES, None),
    )
    return jax.shard_map(
        shards,
        mesh=fine,
        in_specs=placed,
        out_specs=P(FREQ_AXES, SHOT_AXES, None),
        check_vma=False,
    )
```

time: 233 us -> 149 us (0.64)
  waiting for transfers between devices: 131 us -> 49.7 us
  blocking collectives: 34 us -> 0 us
  starting transfers between devices: 22.9 us -> 52.1 us
  between operations: 13.5 us -> 0.37 us
  Pallas kernels: 13.7 us -> 24.6 us
  other arithmetic: 0.32 us -> 4.38 us
    all_gather x2 -> x0, waiting for transfers between devices: 67.4 us -> none  [the longest x1 37.1 us: shards(): g2 = lax.all_gather(swapped_window, 'z', axis=0)]
    all_to_all x1 -> x0, blocking collectives: 34 us -> none  [shards(): arrived = lax.all_to_all(outgoing, SHOT_AXES, 0, 0, tiled=True)]
    ppermute x4 -> x21, starting transfers between devices: 12.1 us -> 34.3 us  [the longest x4 12.4 us: shards(): far[-step] = lax.ppermute(far[1 - step], 'z', left)]
    ppermute x4 -> x21, waiting for transfers between devices: 45.3 us -> 25.3 us  [the longest x3 10.8 us: shards(): far[step] = lax.ppermute(far[step - 1], 'z', right)]
    pallas_call x2 -> x8, Pallas kernels: 13.7 us -> 24.6 us  [the longest x2 12.3 us: product(): pl.pallas_call(kernel, out_shape=jax.ShapeDtypeStruct((2, size, WINDOW),...]
    all_to_all x2, starting transfers between devices: 10.8 us -> 17.8 us  [the longest x1 10.4 us: shards(): arrived = lax.all_to_all(rows, SHOT_AXES + FREQ_AXES, 0, 0, tiled=True)]
    all_to_all x2, waiting for transfers between devices: 18.5 us -> 24.4 us  [the longest x1 16.3 us: shards(): arrived = lax.all_to_all(rows, SHOT_AXES + FREQ_AXES, 0, 0, tiled=True)]
    slice x2 -> x15, local copies, waits for them, and re-layouts: 5.18 us -> 9.4 us  [the longest x8 4.71 us: shards(): strips = [near[d][CHUNK:CHUNK + 1] for d in distances]]
  transfers between devices with their start and end apart: 8 -> 23, of which waited for: 6 -> 12; matrix products, arithmetic and copies ran while one was open for 3% -> 9% of each run, Pallas kernels for 0% -> 11%
where the time goes in v2:
time: 149 us
  starting transfers between devices  52.1 us (35%)
  waiting for transfers between devices  49.7 us (33%)
  Pallas kernels  24.6 us (17%)
  local copies, waits for them, and re-layouts  17.3 us (12%)
  other arithmetic  4.38 us (3%)
    all_to_all x1, waiting for transfers between devices, shards(): arrived = lax.all_to_all(rows, SHOT_AXES + FREQ_AXES, 0, 0, tiled=True)  16.3 us
    ppermute x4, starting transfers between devices, shards(): far[-step] = lax.ppermute(far[1 - step], 'z', left)  12.4 us
    pallas_call x2, Pallas kernels, product(): pl.pallas_call(kernel, out_shape=jax.ShapeDtypeStruct((2, size, WINDOW),...  12.3 us
    ppermute x3, waiting for transfers between devices, shards(): far[step] = lax.ppermute(far[step - 1], 'z', right)  10.8 us
    all_to_all x1, starting transfers between devices, shards(): arrived = lax.all_to_all(rows, SHOT_AXES + FREQ_AXES, 0, 0, tiled=True)  10.4 us
    ppermute x3, starting transfers between devices, shards(): near[-step] = lax.ppermute(near[1 - step], 'z', left)  8.88 us
    all_to_all x1, waiting for transfers between devices, shards(): spectra = lax.all_to_all(estimate, FREQ_AXES + ('xl',), 0, 0, tiled=True)  8.16 us
    all_to_all x1, starting transfers between devices, shards(): spectra = lax.all_to_all(estimate, FREQ_AXES + ('xl',), 0, 0, tiled=True)  7.39 us
  transfers between devices with their start and end apart: 23, of which 12 were waited for; matrix products, arithmetic and copies ran while one was open for 9% of the time, Pallas kernels for 11%

profile of v2, /device:TPU:1, one launch (start us, length us, event | category | flops | bytes accessed | tf_op | source)
XLA Modules:
  0.0 148.5 jit_solution(18051395712253087286)
XLA Ops:
  0.7 2.2 %copy-done = bf16[2,2,128,4096]{3,2,1,0:T(8,128)(2,1)S(1)} copy-done((bf16[2,2,128,4096]{3,2,1,0:T(8,128)(2,1)S(1)}, bf16[2,2,128,4096]{3,2,1,0:T(8,128)(2,1)}, u32[]{:S(2)}) %copy-start) | copy-done | bytes 4194328
  3.8 2.1 %collective-permute-start.2 = (bf16[1040,128]{1,0:T(8,128)(2,1)S(1)}, bf16[1040,128]{1,0:T(8,128)(2,1)S(1)}, u32[]{:S(2)}, u32[]{:S(2)}) collective-permute-start(bf16[1040,128]{1,0:T(8,128)(2,1)S(1)} %get-tuple-element.12), channel_id=1, source_target_pairs={{0,128},{128,0},{1,129},{129,1},{2,130},{130,2},{3,131},{131,3},{4... | collective-permute-start | bytes 798728 | tf_op jit(solution)/shard_map/ppermute | solution.py:371
  6.0 5.6 %collective-permute-start.3 = (bf16[1040,128]{1,0:T(8,128)(2,1)S(1)}, bf16[1040,128]{1,0:T(8,128)(2,1)S(1)}, u32[]{:S(2)}, u32[]{:S(2)}) collective-permute-start(bf16[1040,128]{1,0:T(8,128)(2,1)S(1)} %get-tuple-element.13.refs_0_), channel_id=1, source_target_pairs={{0,112},{16,0},{32,16},{48,32},{64,48},{80,64},{96,80},{112,96},{1... | collective-permute-start | bytes 798728 | tf_op jit(solution)/shard_map/ppermute | solution.py:383
  11.5 3.7 %shard_map.73 = (bf16[2,128,1792]{2,1,0:T(8,128)(2,1)}, bf16[2,128,1792]{2,1,0:T(8,128)(2,1)S(1)}, bf16[2,128,2048]{2,1,0:T(8,128)(2,1)S(1)}) custom-call(s32[3]{0:T(128)S(1)} %pad_add_fusion.place, bf16[2,2,128,4096]{3,2,1,0:T(8,128)(2,1)} %line_in.1), custom_call_target="tpu_custom_call" | custom-call | tf_op jit(solution)/shard_map/pallas_call | solution.py:111
  17.2 1.4 collective-permute-start
  18.6 3.0 %collective-permute-start.10 = (bf16[1040,128]{1,0:T(8,128)(2,1)S(1)}, bf16[1040,128]{1,0:T(8,128)(2,1)S(1)}, u32[]{:S(2)}, u32[]{:S(2)}) collective-permute-start(bf16[1040,128]{1,0:T(8,128)(2,1)S(1)} %collective-permute-done.2.window_in.refs_8_), channel_id=1, source_target_pairs={{0,112},{16,0},{32,16},{48,32},{64,48},{80,64},{96,80},{112,96},{1... | collective-permute-start | bytes 798728 | tf_op jit(solution)/shard_map/ppermute | solution.py:381
  22.0 2.7 %collective-permute-start.5 = (bf16[1040,128]{1,0:T(8,128)(2,1)S(1)}, bf16[1040,128]{1,0:T(8,128)(2,1)S(1)}, u32[]{:S(2)}, u32[]{:S(2)}) collective-permute-start(bf16[1040,128]{1,0:T(8,128)(2,1)S(1)} %collective-permute-done.3.refs_1_), channel_id=1, source_target_pairs={{0,112},{16,0},{32,16},{48,32},{64,48},{80,64},{96,80},{112,96},{1... | collective-permute-start | bytes 798728 | tf_op jit(solution)/shard_map/ppermute | solution.py:383
  24.7 2.8 %collective-permute-done.10.refs_9_ = bf16[1040,128]{1,0:T(8,128)(2,1)S(1)} collective-permute-done((bf16[1040,128]{1,0:T(8,128)(2,1)S(1)}, bf16[1040,128]{1,0:T(8,128)(2,1)S(1)}, u32[]{:S(2)}, u32[]{:S(2)}) %collective-permute-start.10) | collective-permute-done | bytes 266272 | tf_op jit(solution)/shard_map/ppermute | solution.py:381
  27.4 3.4 %collective-permute-start.12 = (bf16[1040,128]{1,0:T(8,128)(2,1)S(1)}, bf16[1040,128]{1,0:T(8,128)(2,1)S(1)}, u32[]{:S(2)}, u32[]{:S(2)}) collective-permute-start(bf16[1040,128]{1,0:T(8,128)(2,1)S(1)} %collective-permute-done.10.refs_9_), channel_id=1, source_target_pairs={{0,112},{16,0},{32,16},{48,32},{64,48},{80,64},{96,80},{112,96},{1... | collective-permute-start | bytes 798728 | tf_op jit(solution)/shard_map/ppermute | solution.py:381
  30.9 2.2 %collective-permute-done.5.refs_3_ = bf16[1040,128]{1,0:T(8,128)(2,1)S(1)} collective-permute-done((bf16[1040,128]{1,0:T(8,128)(2,1)S(1)}, bf16[1040,128]{1,0:T(8,128)(2,1)S(1)}, u32[]{:S(2)}, u32[]{:S(2)}) %collective-permute-start.5) | collective-permute-done | bytes 266272 | tf_op jit(solution)/shard_map/ppermute | solution.py:383
  34.2 2.6 %collective-permute-done.6.refs_4_ = bf16[1040,128]{1,0:T(8,128)(2,1)S(1)} collective-permute-done((bf16[1040,128]{1,0:T(8,128)(2,1)S(1)}, bf16[1040,128]{1,0:T(8,128)(2,1)S(1)}, u32[]{:S(2)}, u32[]{:S(2)}) %collective-permute-start.6) | collective-permute-done | bytes 266272 | tf_op jit(solution)/shard_map/ppermute | solution.py:380
  36.8 2.0 %collective-permute-done.12.refs_11_ = bf16[1040,128]{1,0:T(8,128)(2,1)S(1)} collective-permute-done((bf16[1040,128]{1,0:T(8,128)(2,1)S(1)}, bf16[1040,128]{1,0:T(8,128)(2,1)S(1)}, u32[]{:S(2)}, u32[]{:S(2)}) %collective-permute-start.12) | collective-permute-done | bytes 266272 | tf_op jit(solution)/shard_map/ppermute | solution.py:381
  38.8 3.4 %collective-permute-start.14 = (bf16[1040,128]{1,0:T(8,128)(2,1)S(1)}, bf16[1040,128]{1,0:T(8,128)(2,1)S(1)}, u32[]{:S(2)}, u32[]{:S(2)}) collective-permute-start(bf16[1040,128]{1,0:T(8,128)(2,1)S(1)} %collective-permute-done.12.refs_11_), channel_id=1, source_target_pairs={{0,112},{16,0},{32,16},{48,32},{64,48},{80,64},{96,80},{112,96},{1... | collective-permute-start | bytes 798728 | tf_op jit(solution)/shard_map/ppermute | solution.py:381
  42.4 1.1 collective-permute-start.17
  43.4 1.4 collective-permute-done.8.refs_6_
  45.5 5.1 %collective-permute-done.13.refs_12_ = bf16[1040,128]{1,0:T(8,128)(2,1)S(1)} collective-permute-done((bf16[1040,128]{1,0:T(8,128)(2,1)S(1)}, bf16[1040,128]{1,0:T(8,128)(2,1)S(1)}, u32[]{:S(2)}, u32[]{:S(2)}) %collective-permute-start.13) | collective-permute-done | bytes 266272 | tf_op jit(solution)/shard_map/ppermute | solution.py:384
  50.7 2.7 %collective-permute-start.16 = (bf16[1040,128]{1,0:T(8,128)(2,1)S(1)}, bf16[1040,128]{1,0:T(8,128)(2,1)}, u32[]{:S(2)}, u32[]{:S(2)}) collective-permute-start(bf16[1040,128]{1,0:T(8,128)(2,1)S(1)} %collective-permute-done.14.refs_13_), channel_id=1, source_target_pairs={{0,112},{16,0},{32,16},{48,32},{64,48},{80,64},{96,80},{112,96},{1... | collective-permute-start | bytes 798728 | tf_op jit(solution)/shard_map/ppermute | solution.py:381
  53.4 1.9 %collective-permute-start.1 = (bf16[2,128,1792]{2,1,0:T(8,128)(2,1)}, bf16[2,128,1792]{2,1,0:T(8,128)(2,1)S(1)}, u32[]{:S(2)}, u32[]{:S(2)}) collective-permute-start(bf16[2,128,1792]{2,1,0:T(8,128)(2,1)} %shard_map.74), channel_id=1, source_target_pairs={{0,128},{128,0},{1,129},{129,1},{2,130},{130,2},{3,131},{131,3},{4... | collective-permute-start | bytes 2752520 | tf_op jit(solution)/shard_map/ppermute | solution.py:375
  55.3 2.7 %collective-permute-done.9.refs_7_ = bf16[1040,128]{1,0:T(8,128)(2,1)} collective-permute-done((bf16[1040,128]{1,0:T(8,128)(2,1)S(1)}, bf16[1040,128]{1,0:T(8,128)(2,1)}, u32[]{:S(2)}, u32[]{:S(2)}) %collective-permute-start.9) | collective-permute-done | bytes 266272 | tf_op jit(solution)/shard_map/ppermute | solution.py:380
  57.9 5.7 %collective-permute-done.15.refs_14_ = bf16[1040,128]{1,0:T(8,128)(2,1)} collective-permute-done((bf16[1040,128]{1,0:T(8,128)(2,1)S(1)}, bf16[1040,128]{1,0:T(8,128)(2,1)}, u32[]{:S(2)}, u32[]{:S(2)}) %collective-permute-start.15) | collective-permute-done | bytes 266272 | tf_op jit(solution)/shard_map/ppermute | solution.py:384
  63.6 6.2 %shard_map.77 = f32[2,256,512]{2,1,0:T(8,128)} custom-call(s32[3]{0:T(128)S(1)} %pad_add_fusion.place, bf16[2,128,2048]{2,1,0:T(8,128)(2,1)} %collective-permute-done.17.line_in, bf16[2,128,1792]{2,1,0:T(8,128)(2,1)} %collective-permute-done.earlier.rest_in, bf16[1040,128]{1,0:T(8,128)(2,1)} %collective-permute-done.18.window_in, ...), custom_call_target="tpu_custom_call" | custom-call | flops 2147483648 | bytes 4194304 | tf_op jit(solution)/shard_map/pallas_call | solution.py:218
  69.8 2.9 %collective-permute-start.19 = (f32[2,256,512]{2,1,0:T(8,128)}, f32[2,256,512]{2,1,0:T(8,128)S(1)}, u32[]{:S(2)}, u32[]{:S(2)}) collective-permute-start(f32[2,256,512]{2,1,0:T(8,128)} %shard_map.77), channel_id=1, source_target_pairs={{0,8},{8,0},{1,9},{9,1},{2,10},{10,2},{3,11},{11,3},{4,12},{12,4},... | collective-permute-start | bytes 3145736 | tf_op jit(solution)/shard_map/ppermute | solution.py:387
  74.9 6.2 %shard_map.76.keep = f32[2,256,512]{2,1,0:T(8,128)} custom-call(s32[3]{0:T(128)S(1)} %pad_add_fusion.place, bf16[2,2,128,4096]{3,2,1,0:T(8,128)(2,1)} %line_in.1, bf16[2,128,1792]{2,1,0:T(8,128)(2,1)S(1)} %collective-permute-done.1.rest_in, bf16[1040,128]{1,0:T(8,128)(2,1)S(1)} %collective-permute-done.2.window_in.refs_8_, ...), custom_call_target="tpu_custom_call" | custom-call | flops 2147483648 | bytes 4194304 | tf_op jit(solution)/shard_map/pallas_call | solution.py:218
  81.1 1.2 copy-done.1
  82.3 1.7 %shard_map.78 = bf16[16,32,512]{2,1,0:T(8,128)(2,1)} custom-call(s32[3]{0:T(128)S(1)} %pad_add_fusion.place, f32[2,2]{1,0:T(2,128)S(1)} %copy-done.15, f32[2,256,512]{2,1,0:T(8,128)S(1)} %copy-done.1, f32[2,256,512]{2,1,0:T(8,128)S(1)} %collective-permute-done.19.came, bf16[128,128]{1,0:T(8,128)(2,1)S(1)} %get-tuple-element.22.order_own, ...), custom_call_target="tpu_custom_call" | custom-call | tf_op jit(solution)/shard_map/pallas_call | solution.py:266
  84.0 7.4 %all-to-all-start = ((bf16[16,32,512]{2,1,0:T(8,128)(2,1)}), bf16[16,32,512]{2,1,0:T(8,128)(2,1)S(1)}, u32[]{:S(2)}, u32[]{:S(2)}) async-start(bf16[16,32,512]{2,1,0:T(8,128)(2,1)} %shard_map.78), calls=%async_computation | async-start | bytes 1048576 | tf_op jit(solution)/shard_map/all_to_all | solution.py:414
  92.2 8.2 %all-to-all-done.spectra = bf16[16,32,512]{2,1,0:T(8,128)(2,1)S(1)} async-done(((bf16[16,32,512]{2,1,0:T(8,128)(2,1)}), bf16[16,32,512]{2,1,0:T(8,128)(2,1)S(1)}, u32[]{:S(2)}, u32[]{:S(2)}) %all-to-all-start) | async-done | bytes 524320 | tf_op jit(solution)/shard_map/all_to_all | solution.py:414
  101.4 4.3 %shard_map.79 = bf16[128,2,16,128]{3,2,1,0:T(8,128)(2,1)} custom-call(bf16[16,32,512]{2,1,0:T(8,128)(2,1)S(1)} %all-to-all-done.spectra, bf16[512,512]{1,0:T(8,128)(2,1)S(1)} %copy-done.2, bf16[512,512]{1,0:T(8,128)(2,1)S(1)} %copy-done.3, s32[16,512]{1,0:T(8,128)S(1)} %select_reduce_fusion.trace_map, bf16[1024,512]{1,0:T(8,128)(2,1)S(1)} %get-tuple-element.23.spread, ...), custom_call_target="tpu_custom_call" | custom-call | tf_op jit(solution)/shard_map/pallas_call | solution.py:299
  105.7 10.4 %all-to-all-start.1 = ((bf16[256,16,128]{2,1,0:T(8,128)(2,1)}), bf16[256,16,128]{2,1,0:T(8,128)(2,1)S(1)}, u32[]{:S(2)}, u32[]{:S(2)}) async-start(bf16[256,16,128]{2,1,0:T(8,128)(2,1)} %bitcast.6), calls=%async_computation.1 | async-start | bytes 2097152 | tf_op jit(solution)/shard_map/all_to_all | solution.py:417
  125.9 2.4 %collective-permute-start.20 = (bf16[16,128]{1,0:T(8,128)(2,1)S(1)}, bf16[16,128]{1,0:T(8,128)(2,1)S(1)}, u32[]{:S(2)}, u32[]{:S(2)}) collective-permute-start(bf16[16,128]{1,0:T(8,128)(2,1)S(1)} %concatenate.15), channel_id=1, source_target_pairs={{0,8},{8,0},{1,9},{9,1},{2,10},{10,2},{3,11},{11,3},{4,12},{12,4},... | collective-permute-start | bytes 12296 | tf_op jit(solution)/shard_map/ppermute | solution.py:395
  130.6 16.3 %all-to-all-done.1.arrived = bf16[256,16,128]{2,1,0:T(8,128)(2,1)S(1)} async-done(((bf16[256,16,128]{2,1,0:T(8,128)(2,1)}), bf16[256,16,128]{2,1,0:T(8,128)(2,1)S(1)}, u32[]{:S(2)}, u32[]{:S(2)}) %all-to-all-start.1) | async-done | bytes 1048608 | tf_op jit(solution)/shard_map/all_to_all | solution.py:417
  146.9 1.7 %shard_map.80 = bf16[4,256,512]{2,1,0:T(8,128)(2,1)} custom-call(bf16[256,16,128]{2,1,0:T(8,128)(2,1)S(1)} %all-to-all-done.1.arrived, bf16[16,256,256]{2,1,0:T(8,128)(2,1)S(1)} %fusion.turns), custom_call_target="tpu_custom_call" | custom-call | tf_op jit(solution)/shard_map/pallas_call | solution.py:320
  (117 shorter events, 22.0 us)
Async XLA Ops:
  3.8 70.0 %copy-start.6 = (bf16[1040,128]{1,0:T(8,128)(2,1)}, bf16[1040,128]{1,0:T(8,128)(2,1)S(1)}, u32[]{:S(2)}) copy-start(bf16[1040,128]{1,0:T(8,128)(2,1)S(1)} %get-tuple-element.13.refs_0_) | copy-start | bytes 798724
  3.8 14.7 %collective-permute-start.2 = (bf16[1040,128]{1,0:T(8,128)(2,1)S(1)}, bf16[1040,128]{1,0:T(8,128)(2,1)S(1)}, u32[]{:S(2)}, u32[]{:S(2)}) collective-permute-start(bf16[1040,128]{1,0:T(8,128)(2,1)S(1)} %get-tuple-element.12), channel_id=1, source_target_pairs={{0,128},{128,0},{1,129},{129,1},{2,130},{130,2},{3,131},{131,3},{4... | collective-permute-start | bytes 798728 | tf_op jit(solution)/shard_map/ppermute | solution.py:371
  6.0 16.0 %collective-permute-start.3 = (bf16[1040,128]{1,0:T(8,128)(2,1)S(1)}, bf16[1040,128]{1,0:T(8,128)(2,1)S(1)}, u32[]{:S(2)}, u32[]{:S(2)}) collective-permute-start(bf16[1040,128]{1,0:T(8,128)(2,1)S(1)} %get-tuple-element.13.refs_0_), channel_id=1, source_target_pairs={{0,112},{16,0},{32,16},{48,32},{64,48},{80,64},{96,80},{112,96},{1... | collective-permute-start | bytes 798728 | tf_op jit(solution)/shard_map/ppermute | solution.py:383
  11.5 13.1 %collective-permute-start.4 = (bf16[1040,128]{1,0:T(8,128)(2,1)S(1)}, bf16[1040,128]{1,0:T(8,128)(2,1)S(1)}, u32[]{:S(2)}, u32[]{:S(2)}) collective-permute-start(bf16[1040,128]{1,0:T(8,128)(2,1)S(1)} %get-tuple-element.13.refs_0_), channel_id=1, source_target_pairs={{0,16},{16,32},{32,48},{48,64},{64,80},{80,96},{96,112},{112,0},{1... | collective-permute-start | bytes 798728 | tf_op jit(solution)/shard_map/ppermute | solution.py:380
  17.2 33.4 %collective-permute-start = (bf16[2,128,1792]{2,1,0:T(8,128)(2,1)}, bf16[2,128,1792]{2,1,0:T(8,128)(2,1)}, u32[]{:S(2)}, u32[]{:S(2)}) collective-permute-start(bf16[2,128,1792]{2,1,0:T(8,128)(2,1)} %get-tuple-element.11), channel_id=1, source_target_pairs={{0,136},{8,128},{128,8},{136,0},{1,137},{9,129},{129,9},{137,1},{2... | collective-permute-start | bytes 2752520 | tf_op jit(solution)/shard_map/ppermute | solution.py:373
  18.6 8.8 %collective-permute-start.10 = (bf16[1040,128]{1,0:T(8,128)(2,1)S(1)}, bf16[1040,128]{1,0:T(8,128)(2,1)S(1)}, u32[]{:S(2)}, u32[]{:S(2)}) collective-permute-start(bf16[1040,128]{1,0:T(8,128)(2,1)S(1)} %collective-permute-done.2.window_in.refs_8_), channel_id=1, source_target_pairs={{0,112},{16,0},{32,16},{48,32},{64,48},{80,64},{96,80},{112,96},{1... | collective-permute-start | bytes 798728 | tf_op jit(solution)/shard_map/ppermute | solution.py:381
  21.9 14.8 %collective-permute-start.11 = (bf16[1040,128]{1,0:T(8,128)(2,1)S(1)}, bf16[1040,128]{1,0:T(8,128)(2,1)S(1)}, u32[]{:S(2)}, u32[]{:S(2)}) collective-permute-start(bf16[1040,128]{1,0:T(8,128)(2,1)S(1)} %collective-permute-done.2.window_in.refs_8_), channel_id=1, source_target_pairs={{0,16},{16,32},{32,48},{48,64},{64,80},{80,96},{96,112},{112,0},{1... | collective-permute-start | bytes 798728 | tf_op jit(solution)/shard_map/ppermute | solution.py:384
  22.0 11.1 %collective-permute-start.5 = (bf16[1040,128]{1,0:T(8,128)(2,1)S(1)}, bf16[1040,128]{1,0:T(8,128)(2,1)S(1)}, u32[]{:S(2)}, u32[]{:S(2)}) collective-permute-start(bf16[1040,128]{1,0:T(8,128)(2,1)S(1)} %collective-permute-done.3.refs_1_), channel_id=1, source_target_pairs={{0,112},{16,0},{32,16},{48,32},{64,48},{80,64},{96,80},{112,96},{1... | collective-permute-start | bytes 798728 | tf_op jit(solution)/shard_map/ppermute | solution.py:383
  24.7 49.2 %copy-start.4 = (bf16[1040,128]{1,0:T(8,128)(2,1)}, bf16[1040,128]{1,0:T(8,128)(2,1)S(1)}, u32[]{:S(2)}) copy-start(bf16[1040,128]{1,0:T(8,128)(2,1)S(1)} %collective-permute-done.4.refs_2_) | copy-start | bytes 798724
  24.7 12.1 %collective-permute-start.6 = (bf16[1040,128]{1,0:T(8,128)(2,1)S(1)}, bf16[1040,128]{1,0:T(8,128)(2,1)S(1)}, u32[]{:S(2)}, u32[]{:S(2)}) collective-permute-start(bf16[1040,128]{1,0:T(8,128)(2,1)S(1)} %collective-permute-done.4.refs_2_), channel_id=1, source_target_pairs={{0,16},{16,32},{32,48},{48,64},{64,80},{80,96},{96,112},{112,0},{1... | collective-permute-start | bytes 798728 | tf_op jit(solution)/shard_map/ppermute | solution.py:380
  27.4 46.4 %copy-start.5 = (bf16[1040,128]{1,0:T(8,128)(2,1)}, bf16[1040,128]{1,0:T(8,128)(2,1)S(1)}, u32[]{:S(2)}) copy-start(bf16[1040,128]{1,0:T(8,128)(2,1)S(1)} %collective-permute-done.10.refs_9_) | copy-start | bytes 798724
  27.4 11.4 %collective-permute-start.12 = (bf16[1040,128]{1,0:T(8,128)(2,1)S(1)}, bf16[1040,128]{1,0:T(8,128)(2,1)S(1)}, u32[]{:S(2)}, u32[]{:S(2)}) collective-permute-start(bf16[1040,128]{1,0:T(8,128)(2,1)S(1)} %collective-permute-done.10.refs_9_), channel_id=1, source_target_pairs={{0,112},{16,0},{32,16},{48,32},{64,48},{80,64},{96,80},{112,96},{1... | collective-permute-start | bytes 798728 | tf_op jit(solution)/shard_map/ppermute | solution.py:381
  33.1 40.7 %copy-start.8 = (bf16[1040,128]{1,0:T(8,128)(2,1)}, bf16[1040,128]{1,0:T(8,128)(2,1)S(1)}, u32[]{:S(2)}) copy-start(bf16[1040,128]{1,0:T(8,128)(2,1)S(1)} %collective-permute-done.5.refs_3_) | copy-start | bytes 798724
  33.1 9.3 %collective-permute-start.18 = (bf16[1040,128]{1,0:T(8,128)(2,1)S(1)}, bf16[1040,128]{1,0:T(8,128)(2,1)}, u32[]{:S(2)}, u32[]{:S(2)}) collective-permute-start(bf16[1040,128]{1,0:T(8,128)(2,1)S(1)} %collective-permute-done.2.window_in.refs_8_), channel_id=1, source_target_pairs={{0,8},{8,0},{1,9},{9,1},{2,10},{10,2},{3,11},{11,3},{4,12},{12,4},... | collective-permute-start | bytes 798728 | tf_op jit(solution)/shard_map/ppermute | solution.py:376
  36.7 37.1 %copy-start.10 = (bf16[1040,128]{1,0:T(8,128)(2,1)}, bf16[1040,128]{1,0:T(8,128)(2,1)S(1)}, u32[]{:S(2)}) copy-start(bf16[1040,128]{1,0:T(8,128)(2,1)S(1)} %collective-permute-done.6.refs_4_) | copy-start | bytes 798724
  36.7 8.1 %collective-permute-start.8 = (bf16[1040,128]{1,0:T(8,128)(2,1)S(1)}, bf16[1040,128]{1,0:T(8,128)(2,1)S(1)}, u32[]{:S(2)}, u32[]{:S(2)}) collective-permute-start(bf16[1040,128]{1,0:T(8,128)(2,1)S(1)} %collective-permute-done.6.refs_4_), channel_id=1, source_target_pairs={{0,16},{16,32},{32,48},{48,64},{64,80},{80,96},{96,112},{112,0},{1... | collective-permute-start | bytes 798728 | tf_op jit(solution)/shard_map/ppermute | solution.py:380
  36.7 37.1 %copy-start.7 = (bf16[1040,128]{1,0:T(8,128)(2,1)}, bf16[1040,128]{1,0:T(8,128)(2,1)S(1)}, u32[]{:S(2)}) copy-start(bf16[1040,128]{1,0:T(8,128)(2,1)S(1)} %collective-permute-done.11.refs_10_) | copy-start | bytes 798724
  36.8 13.8 %collective-permute-start.13 = (bf16[1040,128]{1,0:T(8,128)(2,1)S(1)}, bf16[1040,128]{1,0:T(8,128)(2,1)S(1)}, u32[]{:S(2)}, u32[]{:S(2)}) collective-permute-start(bf16[1040,128]{1,0:T(8,128)(2,1)S(1)} %collective-permute-done.11.refs_10_), channel_id=1, source_target_pairs={{0,16},{16,32},{32,48},{48,64},{64,80},{80,96},{96,112},{112,0},{1... | collective-permute-start | bytes 798728 | tf_op jit(solution)/shard_map/ppermute | solution.py:384
  38.8 35.1 %copy-start.9 = (bf16[1040,128]{1,0:T(8,128)(2,1)}, bf16[1040,128]{1,0:T(8,128)(2,1)S(1)}, u32[]{:S(2)}) copy-start(bf16[1040,128]{1,0:T(8,128)(2,1)S(1)} %collective-permute-done.12.refs_11_) | copy-start | bytes 798724
  38.8 11.9 %collective-permute-start.14 = (bf16[1040,128]{1,0:T(8,128)(2,1)S(1)}, bf16[1040,128]{1,0:T(8,128)(2,1)S(1)}, u32[]{:S(2)}, u32[]{:S(2)}) collective-permute-start(bf16[1040,128]{1,0:T(8,128)(2,1)S(1)} %collective-permute-done.12.refs_11_), channel_id=1, source_target_pairs={{0,112},{16,0},{32,16},{48,32},{64,48},{80,64},{96,80},{112,96},{1... | collective-permute-start | bytes 798728 | tf_op jit(solution)/shard_map/ppermute | solution.py:381
  42.4 12.9 %collective-permute-start.17 = (bf16[2,128,2048]{2,1,0:T(8,128)(2,1)}, bf16[2,128,2048]{2,1,0:T(8,128)(2,1)}, u32[]{:S(2)}, u32[]{:S(2)}) collective-permute-start(bf16[2,128,2048]{2,1,0:T(8,128)(2,1)} %copy-done.16), channel_id=1, source_target_pairs={{0,8},{8,0},{1,9},{9,1},{2,10},{10,2},{3,11},{11,3},{4,12},{12,4},... | collective-permute-start | bytes 3145736 | tf_op jit(solution)/shard_map/ppermute | solution.py:374
  44.9 29.0 %copy-start.11 = (bf16[1040,128]{1,0:T(8,128)(2,1)}, bf16[1040,128]{1,0:T(8,128)(2,1)S(1)}, u32[]{:S(2)}) copy-start(bf16[1040,128]{1,0:T(8,128)(2,1)S(1)} %collective-permute-done.8.refs_6_) | copy-start | bytes 798724
  44.9 8.5 %collective-permute-start.7 = (bf16[1040,128]{1,0:T(8,128)(2,1)S(1)}, bf16[1040,128]{1,0:T(8,128)(2,1)}, u32[]{:S(2)}, u32[]{:S(2)}) collective-permute-start(bf16[1040,128]{1,0:T(8,128)(2,1)S(1)} %collective-permute-done.5.refs_3_), channel_id=1, source_target_pairs={{0,112},{16,0},{32,16},{48,32},{64,48},{80,64},{96,80},{112,96},{1... | collective-permute-start | bytes 798728 | tf_op jit(solution)/shard_map/ppermute | solution.py:383
  50.6 7.3 %collective-permute-start.9 = (bf16[1040,128]{1,0:T(8,128)(2,1)S(1)}, bf16[1040,128]{1,0:T(8,128)(2,1)}, u32[]{:S(2)}, u32[]{:S(2)}) collective-permute-start(bf16[1040,128]{1,0:T(8,128)(2,1)S(1)} %collective-permute-done.8.refs_6_), channel_id=1, source_target_pairs={{0,16},{16,32},{32,48},{48,64},{64,80},{80,96},{96,112},{112,0},{1... | collective-permute-start | bytes 798728 | tf_op jit(solution)/shard_map/ppermute | solution.py:380
  50.6 13.0 %collective-permute-start.15 = (bf16[1040,128]{1,0:T(8,128)(2,1)S(1)}, bf16[1040,128]{1,0:T(8,128)(2,1)}, u32[]{:S(2)}, u32[]{:S(2)}) collective-permute-start(bf16[1040,128]{1,0:T(8,128)(2,1)S(1)} %collective-permute-done.13.refs_12_), channel_id=1, source_target_pairs={{0,16},{16,32},{32,48},{48,64},{64,80},{80,96},{96,112},{112,0},{1... | collective-permute-start | bytes 798728 | tf_op jit(solution)/shard_map/ppermute | solution.py:384
  50.7 12.9 %collective-permute-start.16 = (bf16[1040,128]{1,0:T(8,128)(2,1)S(1)}, bf16[1040,128]{1,0:T(8,128)(2,1)}, u32[]{:S(2)}, u32[]{:S(2)}) collective-permute-start(bf16[1040,128]{1,0:T(8,128)(2,1)S(1)} %collective-permute-done.14.refs_13_), channel_id=1, source_target_pairs={{0,112},{16,0},{32,16},{48,32},{64,48},{80,64},{96,80},{112,96},{1... | collective-permute-start | bytes 798728 | tf_op jit(solution)/shard_map/ppermute | solution.py:381
  53.4 20.5 %collective-permute-start.1 = (bf16[2,128,1792]{2,1,0:T(8,128)(2,1)}, bf16[2,128,1792]{2,1,0:T(8,128)(2,1)S(1)}, u32[]{:S(2)}, u32[]{:S(2)}) collective-permute-start(bf16[2,128,1792]{2,1,0:T(8,128)(2,1)} %shard_map.74), channel_id=1, source_target_pairs={{0,128},{128,0},{1,129},{129,1},{2,130},{130,2},{3,131},{131,3},{4... | collective-permute-start | bytes 2752520 | tf_op jit(solution)/shard_map/ppermute | solution.py:375
  69.8 11.2 %collective-permute-start.19 = (f32[2,256,512]{2,1,0:T(8,128)}, f32[2,256,512]{2,1,0:T(8,128)S(1)}, u32[]{:S(2)}, u32[]{:S(2)}) collective-permute-start(f32[2,256,512]{2,1,0:T(8,128)} %shard_map.77), channel_id=1, source_target_pairs={{0,8},{8,0},{1,9},{9,1},{2,10},{10,2},{3,11},{11,3},{4,12},{12,4},... | collective-permute-start | bytes 3145736 | tf_op jit(solution)/shard_map/ppermute | solution.py:387
  74.9 25.5 %copy-start.2 = (bf16[512,512]{1,0:T(8,128)(2,1)S(1)}, bf16[512,512]{1,0:T(8,128)(2,1)}, u32[]{:S(2)}) copy-start(bf16[512,512]{1,0:T(8,128)(2,1)} %constant.127.clone.high) | copy-start | bytes 1572868
  84.0 16.4 %all-to-all-start = ((bf16[16,32,512]{2,1,0:T(8,128)(2,1)}), bf16[16,32,512]{2,1,0:T(8,128)(2,1)S(1)}, u32[]{:S(2)}, u32[]{:S(2)}) async-start(bf16[16,32,512]{2,1,0:T(8,128)(2,1)} %shard_map.78), calls=%async_computation | async-start | bytes 1048576 | tf_op jit(solution)/shard_map/all_to_all | solution.py:414
  105.7 41.1 %all-to-all-start.1 = ((bf16[256,16,128]{2,1,0:T(8,128)(2,1)}), bf16[256,16,128]{2,1,0:T(8,128)(2,1)S(1)}, u32[]{:S(2)}, u32[]{:S(2)}) async-start(bf16[256,16,128]{2,1,0:T(8,128)(2,1)} %bitcast.6), calls=%async_computation.1 | async-start | bytes 2097152 | tf_op jit(solution)/shard_map/all_to_all | solution.py:417
  125.9 3.3 %collective-permute-start.20 = (bf16[16,128]{1,0:T(8,128)(2,1)S(1)}, bf16[16,128]{1,0:T(8,128)(2,1)S(1)}, u32[]{:S(2)}, u32[]{:S(2)}) collective-permute-start(bf16[16,128]{1,0:T(8,128)(2,1)S(1)} %concatenate.15), channel_id=1, source_target_pairs={{0,8},{8,0},{1,9},{9,1},{2,10},{10,2},{3,11},{11,3},{4,12},{12,4},... | collective-permute-start | bytes 12296 | tf_op jit(solution)/shard_map/ppermute | solution.py:395
  (12 other events, 113.1 us)

commit v3 on v2

--- a/solution.py
+++ b/solution.py
@@ -34,7 +34,7 @@
     full = full.reshape(PART_SHOTS * TIMES, 2 * FREQS * PART_SHOTS).astype(np.float32)
     high = full.astype(BF)
     low = (full - high.astype(np.float32)).astype(BF)
-    return high, low
+    return np.concatenate([high, low], axis=0)
 
 
 HBM = pl.BlockSpec(memory_space=pltpu.HBM)
@@ -272,9 +272,10 @@
     )(place, wavelet, keep, came, order_own, order_other)
 
 
-def transform_kernel(spectra, high, low, trace_map, spread, swapped, out, traces, moved):
+def transform_kernel(spectra, tables, trace_map, spread, swapped, out, traces, moved):
     x = spectra[...].reshape(512, WINDOW)
-    traces[...] = (dot(high[...], x) + dot(low[...], x)).astype(BF)
+    both = dot(tables[...], x)
+    traces[...] = (both[:512] + both[512:]).astype(BF)
     receivers = lax.broadcasted_iota(jnp.int32, (WINDOW, WINDOW), 0)
     for shot in range(PART_SHOTS):
         rows = slice(shot * TIMES, (shot + 1) * TIMES)
@@ -295,13 +296,12 @@
 
 
 def transform(spectra, trace_map, spread, swapped):
-    high, low = transform_tables()
     return pl.pallas_call(
         transform_kernel,
         out_shape=jax.ShapeDtypeStruct((128, 2, 16, 128), BF),
         scratch_shapes=[pltpu.VMEM((512, WINDOW), BF)] * 2,
         compiler_params=PARAMS,
-    )(spectra, jnp.asarray(high), jnp.asarray(low), trace_map, spread, swapped)
+    )(spectra, jnp.asarray(transform_tables()), trace_map, spread, swapped)
 
 
 def place_kernel(arrived, turns, out):

time: 149 us -> 148 us (level)
  local copies, waits for them, and re-layouts: 17.3 us -> 15.3 us
    unnamed x42 -> x34, local copies, waits for them, and re-layouts: 7.35 us -> 6.6 us
  transfers between devices with their start and end apart: 23 -> 23, of which waited for: 12 -> 12; matrix products, arithmetic and copies ran while one was open for 9% -> 8% of each run, Pallas kernels for 11% -> 11%
where the time goes in v3:
time: 148 us
  starting transfers between devices  52.1 us (35%)
  waiting for transfers between devices  51 us (34%)
  Pallas kernels  24.7 us (17%)
  local copies, waits for them, and re-layouts  15.3 us (10%)
  other arithmetic  4.38 us (3%)
    all_to_all x1, waiting for transfers between devices, shards(): arrived = lax.all_to_all(rows, SHOT_AXES + FREQ_AXES, 0, 0, tiled=True)  17.6 us
    ppermute x4, starting transfers between devices, shards(): far[-step] = lax.ppermute(far[1 - step], 'z', left)  12.4 us
    pallas_call x2, Pallas kernels, product(): pl.pallas_call(kernel, out_shape=jax.ShapeDtypeStruct((2, size, WINDOW),...  12.4 us
    ppermute x3, waiting for transfers between devices, shards(): far[step] = lax.ppermute(far[step - 1], 'z', right)  10.8 us
    all_to_all x1, starting transfers between devices, shards(): arrived = lax.all_to_all(rows, SHOT_AXES + FREQ_AXES, 0, 0, tiled=True)  10.3 us
    ppermute x3, starting transfers between devices, shards(): near[-step] = lax.ppermute(near[1 - step], 'z', left)  8.88 us
    all_to_all x1, waiting for transfers between devices, shards(): spectra = lax.all_to_all(estimate, FREQ_AXES + ('xl',), 0, 0, tiled=True)  8.16 us
    all_to_all x1, starting transfers between devices, shards(): spectra = lax.all_to_all(estimate, FREQ_AXES + ('xl',), 0, 0, tiled=True)  7.44 us
  transfers between devices with their start and end apart: 23, of which 12 were waited for; matrix products, arithmetic and copies ran while one was open for 8% of the time, Pallas kernels for 11%

profile of v3, /device:TPU:1, one launch (start us, length us, event | category | flops | bytes accessed | tf_op | source)
XLA Modules:
  0.0 147.8 jit_solution(10164651736594229073)
XLA Ops:
  0.7 2.2 %copy-done = bf16[2,2,128,4096]{3,2,1,0:T(8,128)(2,1)S(1)} copy-done((bf16[2,2,128,4096]{3,2,1,0:T(8,128)(2,1)S(1)}, bf16[2,2,128,4096]{3,2,1,0:T(8,128)(2,1)}, u32[]{:S(2)}) %copy-start) | copy-done | bytes 4194328
  3.8 2.1 %collective-permute-start.2 = (bf16[1040,128]{1,0:T(8,128)(2,1)S(1)}, bf16[1040,128]{1,0:T(8,128)(2,1)S(1)}, u32[]{:S(2)}, u32[]{:S(2)}) collective-permute-start(bf16[1040,128]{1,0:T(8,128)(2,1)S(1)} %get-tuple-element.12), channel_id=1, source_target_pairs={{0,128},{128,0},{1,129},{129,1},{2,130},{130,2},{3,131},{131,3},{4... | collective-permute-start | bytes 798728 | tf_op jit(solution)/shard_map/ppermute | solution.py:371
  6.0 5.6 %collective-permute-start.3 = (bf16[1040,128]{1,0:T(8,128)(2,1)S(1)}, bf16[1040,128]{1,0:T(8,128)(2,1)S(1)}, u32[]{:S(2)}, u32[]{:S(2)}) collective-permute-start(bf16[1040,128]{1,0:T(8,128)(2,1)S(1)} %get-tuple-element.13.refs_0_), channel_id=1, source_target_pairs={{0,112},{16,0},{32,16},{48,32},{64,48},{80,64},{96,80},{112,96},{1... | collective-permute-start | bytes 798728 | tf_op jit(solution)/shard_map/ppermute | solution.py:383
  11.5 3.7 %shard_map.64 = (bf16[2,128,1792]{2,1,0:T(8,128)(2,1)}, bf16[2,128,1792]{2,1,0:T(8,128)(2,1)S(1)}, bf16[2,128,2048]{2,1,0:T(8,128)(2,1)S(1)}) custom-call(s32[3]{0:T(128)S(1)} %pad_add_fusion.place, bf16[2,2,128,4096]{3,2,1,0:T(8,128)(2,1)} %line_in.1), custom_call_target="tpu_custom_call" | custom-call | tf_op jit(solution)/shard_map/pallas_call | solution.py:111
  17.2 1.4 collective-permute-start
  18.6 3.0 %collective-permute-start.10 = (bf16[1040,128]{1,0:T(8,128)(2,1)S(1)}, bf16[1040,128]{1,0:T(8,128)(2,1)S(1)}, u32[]{:S(2)}, u32[]{:S(2)}) collective-permute-start(bf16[1040,128]{1,0:T(8,128)(2,1)S(1)} %collective-permute-done.2.window_in.refs_8_), channel_id=1, source_target_pairs={{0,112},{16,0},{32,16},{48,32},{64,48},{80,64},{96,80},{112,96},{1... | collective-permute-start | bytes 798728 | tf_op jit(solution)/shard_map/ppermute | solution.py:381
  22.0 2.7 %collective-permute-start.5 = (bf16[1040,128]{1,0:T(8,128)(2,1)S(1)}, bf16[1040,128]{1,0:T(8,128)(2,1)S(1)}, u32[]{:S(2)}, u32[]{:S(2)}) collective-permute-start(bf16[1040,128]{1,0:T(8,128)(2,1)S(1)} %collective-permute-done.3.refs_1_), channel_id=1, source_target_pairs={{0,112},{16,0},{32,16},{48,32},{64,48},{80,64},{96,80},{112,96},{1... | collective-permute-start | bytes 798728 | tf_op jit(solution)/shard_map/ppermute | solution.py:383
  24.7 2.8 %collective-permute-done.10.refs_9_ = bf16[1040,128]{1,0:T(8,128)(2,1)S(1)} collective-permute-done((bf16[1040,128]{1,0:T(8,128)(2,1)S(1)}, bf16[1040,128]{1,0:T(8,128)(2,1)S(1)}, u32[]{:S(2)}, u32[]{:S(2)}) %collective-permute-start.10) | collective-permute-done | bytes 266272 | tf_op jit(solution)/shard_map/ppermute | solution.py:381
  27.4 3.4 %collective-permute-start.12 = (bf16[1040,128]{1,0:T(8,128)(2,1)S(1)}, bf16[1040,128]{1,0:T(8,128)(2,1)S(1)}, u32[]{:S(2)}, u32[]{:S(2)}) collective-permute-start(bf16[1040,128]{1,0:T(8,128)(2,1)S(1)} %collective-permute-done.10.refs_9_), channel_id=1, source_target_pairs={{0,112},{16,0},{32,16},{48,32},{64,48},{80,64},{96,80},{112,96},{1... | collective-permute-start | bytes 798728 | tf_op jit(solution)/shard_map/ppermute | solution.py:381
  30.9 2.2 %collective-permute-done.5.refs_3_ = bf16[1040,128]{1,0:T(8,128)(2,1)S(1)} collective-permute-done((bf16[1040,128]{1,0:T(8,128)(2,1)S(1)}, bf16[1040,128]{1,0:T(8,128)(2,1)S(1)}, u32[]{:S(2)}, u32[]{:S(2)}) %collective-permute-start.5) | collective-permute-done | bytes 266272 | tf_op jit(solution)/shard_map/ppermute | solution.py:383
  34.2 2.6 %collective-permute-done.6.refs_4_ = bf16[1040,128]{1,0:T(8,128)(2,1)S(1)} collective-permute-done((bf16[1040,128]{1,0:T(8,128)(2,1)S(1)}, bf16[1040,128]{1,0:T(8,128)(2,1)S(1)}, u32[]{:S(2)}, u32[]{:S(2)}) %collective-permute-start.6) | collective-permute-done | bytes 266272 | tf_op jit(solution)/shard_map/ppermute | solution.py:380
  36.9 2.0 %collective-permute-done.12.refs_11_ = bf16[1040,128]{1,0:T(8,128)(2,1)S(1)} collective-permute-done((bf16[1040,128]{1,0:T(8,128)(2,1)S(1)}, bf16[1040,128]{1,0:T(8,128)(2,1)S(1)}, u32[]{:S(2)}, u32[]{:S(2)}) %collective-permute-start.12) | collective-permute-done | bytes 266272 | tf_op jit(solution)/shard_map/ppermute | solution.py:381
  38.9 3.4 %collective-permute-start.14 = (bf16[1040,128]{1,0:T(8,128)(2,1)S(1)}, bf16[1040,128]{1,0:T(8,128)(2,1)S(1)}, u32[]{:S(2)}, u32[]{:S(2)}) collective-permute-start(bf16[1040,128]{1,0:T(8,128)(2,1)S(1)} %collective-permute-done.12.refs_11_), channel_id=1, source_target_pairs={{0,112},{16,0},{32,16},{48,32},{64,48},{80,64},{96,80},{112,96},{1... | collective-permute-start | bytes 798728 | tf_op jit(solution)/shard_map/ppermute | solution.py:381
  43.5 1.4 collective-permute-done.8.refs_6_
  45.6 5.1 %collective-permute-done.13.refs_12_ = bf16[1040,128]{1,0:T(8,128)(2,1)S(1)} collective-permute-done((bf16[1040,128]{1,0:T(8,128)(2,1)S(1)}, bf16[1040,128]{1,0:T(8,128)(2,1)S(1)}, u32[]{:S(2)}, u32[]{:S(2)}) %collective-permute-start.13) | collective-permute-done | bytes 266272 | tf_op jit(solution)/shard_map/ppermute | solution.py:384
  50.7 2.7 %collective-permute-start.16 = (bf16[1040,128]{1,0:T(8,128)(2,1)S(1)}, bf16[1040,128]{1,0:T(8,128)(2,1)}, u32[]{:S(2)}, u32[]{:S(2)}) collective-permute-start(bf16[1040,128]{1,0:T(8,128)(2,1)S(1)} %collective-permute-done.14.refs_13_), channel_id=1, source_target_pairs={{0,112},{16,0},{32,16},{48,32},{64,48},{80,64},{96,80},{112,96},{1... | collective-permute-start | bytes 798728 | tf_op jit(solution)/shard_map/ppermute | solution.py:381
  53.4 1.9 %collective-permute-start.1 = (bf16[2,128,1792]{2,1,0:T(8,128)(2,1)}, bf16[2,128,1792]{2,1,0:T(8,128)(2,1)S(1)}, u32[]{:S(2)}, u32[]{:S(2)}) collective-permute-start(bf16[2,128,1792]{2,1,0:T(8,128)(2,1)} %shard_map.65), channel_id=1, source_target_pairs={{0,128},{128,0},{1,129},{129,1},{2,130},{130,2},{3,131},{131,3},{4... | collective-permute-start | bytes 2752520 | tf_op jit(solution)/shard_map/ppermute | solution.py:375
  55.3 2.7 %collective-permute-done.9.refs_7_ = bf16[1040,128]{1,0:T(8,128)(2,1)} collective-permute-done((bf16[1040,128]{1,0:T(8,128)(2,1)S(1)}, bf16[1040,128]{1,0:T(8,128)(2,1)}, u32[]{:S(2)}, u32[]{:S(2)}) %collective-permute-start.9) | collective-permute-done | bytes 266272 | tf_op jit(solution)/shard_map/ppermute | solution.py:380
  58.0 5.7 %collective-permute-done.15.refs_14_ = bf16[1040,128]{1,0:T(8,128)(2,1)} collective-permute-done((bf16[1040,128]{1,0:T(8,128)(2,1)S(1)}, bf16[1040,128]{1,0:T(8,128)(2,1)}, u32[]{:S(2)}, u32[]{:S(2)}) %collective-permute-start.15) | collective-permute-done | bytes 266272 | tf_op jit(solution)/shard_map/ppermute | solution.py:384
  63.7 6.2 %shard_map.68 = f32[2,256,512]{2,1,0:T(8,128)} custom-call(s32[3]{0:T(128)S(1)} %pad_add_fusion.place, bf16[2,128,2048]{2,1,0:T(8,128)(2,1)} %collective-permute-done.17.line_in, bf16[2,128,1792]{2,1,0:T(8,128)(2,1)} %collective-permute-done.earlier.rest_in, bf16[1040,128]{1,0:T(8,128)(2,1)} %collective-permute-done.18.window_in, ...), custom_call_target="tpu_custom_call" | custom-call | flops 2147483648 | bytes 4194304 | tf_op jit(solution)/shard_map/pallas_call | solution.py:218
  69.9 2.9 %collective-permute-start.19 = (f32[2,256,512]{2,1,0:T(8,128)}, f32[2,256,512]{2,1,0:T(8,128)S(1)}, u32[]{:S(2)}, u32[]{:S(2)}) collective-permute-start(f32[2,256,512]{2,1,0:T(8,128)} %shard_map.68), channel_id=1, source_target_pairs={{0,8},{8,0},{1,9},{9,1},{2,10},{10,2},{3,11},{11,3},{4,12},{12,4},... | collective-permute-start | bytes 3145736 | tf_op jit(solution)/shard_map/ppermute | solution.py:387
  73.9 6.2 %shard_map.67.keep = f32[2,256,512]{2,1,0:T(8,128)} custom-call(s32[3]{0:T(128)S(1)} %pad_add_fusion.place, bf16[2,2,128,4096]{3,2,1,0:T(8,128)(2,1)} %line_in.1, bf16[2,128,1792]{2,1,0:T(8,128)(2,1)S(1)} %collective-permute-done.1.rest_in, bf16[1040,128]{1,0:T(8,128)(2,1)S(1)} %collective-permute-done.2.window_in.refs_8_, ...), custom_call_target="tpu_custom_call" | custom-call | flops 2147483648 | bytes 4194304 | tf_op jit(solution)/shard_map/pallas_call | solution.py:218
  80.1 1.2 copy-done.1
  81.4 1.7 %shard_map.69 = bf16[16,32,512]{2,1,0:T(8,128)(2,1)} custom-call(s32[3]{0:T(128)S(1)} %pad_add_fusion.place, f32[2,2]{1,0:T(2,128)S(1)} %copy-done.11, f32[2,256,512]{2,1,0:T(8,128)S(1)} %copy-done.1, f32[2,256,512]{2,1,0:T(8,128)S(1)} %collective-permute-done.19.came, bf16[128,128]{1,0:T(8,128)(2,1)S(1)} %get-tuple-element.22.order_own, ...), custom_call_target="tpu_custom_call" | custom-call | tf_op jit(solution)/shard_map/pallas_call | solution.py:266
  83.1 7.4 %all-to-all-start = ((bf16[16,32,512]{2,1,0:T(8,128)(2,1)}), bf16[16,32,512]{2,1,0:T(8,128)(2,1)S(1)}, u32[]{:S(2)}, u32[]{:S(2)}) async-start(bf16[16,32,512]{2,1,0:T(8,128)(2,1)} %shard_map.69), calls=%async_computation | async-start | bytes 1048576 | tf_op jit(solution)/shard_map/all_to_all | solution.py:414
  91.4 8.2 %all-to-all-done.spectra = bf16[16,32,512]{2,1,0:T(8,128)(2,1)S(1)} async-done(((bf16[16,32,512]{2,1,0:T(8,128)(2,1)}), bf16[16,32,512]{2,1,0:T(8,128)(2,1)S(1)}, u32[]{:S(2)}, u32[]{:S(2)}) %all-to-all-start) | async-done | bytes 524320 | tf_op jit(solution)/shard_map/all_to_all | solution.py:414
  99.5 1.2 copy-done.2
  100.7 4.3 %shard_map.70 = bf16[128,2,16,128]{3,2,1,0:T(8,128)(2,1)} custom-call(bf16[16,32,512]{2,1,0:T(8,128)(2,1)S(1)} %all-to-all-done.spectra, bf16[1024,512]{1,0:T(8,128)(2,1)S(1)} %copy-done.2, s32[16,512]{1,0:T(8,128)S(1)} %select_reduce_fusion.trace_map, bf16[1024,512]{1,0:T(8,128)(2,1)S(1)} %get-tuple-element.23.spread, ...), custom_call_target="tpu_custom_call" | custom-call | tf_op jit(solution)/shard_map/pallas_call | solution.py:299
  105.0 10.3 %all-to-all-start.1 = ((bf16[256,16,128]{2,1,0:T(8,128)(2,1)}), bf16[256,16,128]{2,1,0:T(8,128)(2,1)S(1)}, u32[]{:S(2)}, u32[]{:S(2)}) async-start(bf16[256,16,128]{2,1,0:T(8,128)(2,1)} %bitcast.6), calls=%async_computation.1 | async-start | bytes 2097152 | tf_op jit(solution)/shard_map/all_to_all | solution.py:417
  123.8 2.4 %collective-permute-start.20 = (bf16[16,128]{1,0:T(8,128)(2,1)S(1)}, bf16[16,128]{1,0:T(8,128)(2,1)S(1)}, u32[]{:S(2)}, u32[]{:S(2)}) collective-permute-start(bf16[16,128]{1,0:T(8,128)(2,1)S(1)} %concatenate.15), channel_id=1, source_target_pairs={{0,8},{8,0},{1,9},{9,1},{2,10},{10,2},{3,11},{11,3},{4,12},{12,4},... | collective-permute-start | bytes 12296 | tf_op jit(solution)/shard_map/ppermute | solution.py:395
  128.5 17.6 %all-to-all-done.1.arrived = bf16[256,16,128]{2,1,0:T(8,128)(2,1)S(1)} async-done(((bf16[256,16,128]{2,1,0:T(8,128)(2,1)}), bf16[256,16,128]{2,1,0:T(8,128)(2,1)S(1)}, u32[]{:S(2)}, u32[]{:S(2)}) %all-to-all-start.1) | async-done | bytes 1048608 | tf_op jit(solution)/shard_map/all_to_all | solution.py:417
  146.1 1.7 %shard_map.71 = bf16[4,256,512]{2,1,0:T(8,128)(2,1)} custom-call(bf16[256,16,128]{2,1,0:T(8,128)(2,1)S(1)} %all-to-all-done.1.arrived, bf16[16,256,256]{2,1,0:T(8,128)(2,1)S(1)} %fusion.turns), custom_call_target="tpu_custom_call" | custom-call | tf_op jit(solution)/shard_map/pallas_call | solution.py:320
  (109 shorter events, 19.8 us)
Async XLA Ops:
  3.8 70.0 %copy-start.3 = (bf16[1040,128]{1,0:T(8,128)(2,1)}, bf16[1040,128]{1,0:T(8,128)(2,1)S(1)}, u32[]{:S(2)}) copy-start(bf16[1040,128]{1,0:T(8,128)(2,1)S(1)} %get-tuple-element.13.refs_0_) | copy-start | bytes 798724
  3.8 14.8 %collective-permute-start.2 = (bf16[1040,128]{1,0:T(8,128)(2,1)S(1)}, bf16[1040,128]{1,0:T(8,128)(2,1)S(1)}, u32[]{:S(2)}, u32[]{:S(2)}) collective-permute-start(bf16[1040,128]{1,0:T(8,128)(2,1)S(1)} %get-tuple-element.12), channel_id=1, source_target_pairs={{0,128},{128,0},{1,129},{129,1},{2,130},{130,2},{3,131},{131,3},{4... | collective-permute-start | bytes 798728 | tf_op jit(solution)/shard_map/ppermute | solution.py:371
  6.0 16.1 %collective-permute-start.3 = (bf16[1040,128]{1,0:T(8,128)(2,1)S(1)}, bf16[1040,128]{1,0:T(8,128)(2,1)S(1)}, u32[]{:S(2)}, u32[]{:S(2)}) collective-permute-start(bf16[1040,128]{1,0:T(8,128)(2,1)S(1)} %get-tuple-element.13.refs_0_), channel_id=1, source_target_pairs={{0,112},{16,0},{32,16},{48,32},{64,48},{80,64},{96,80},{112,96},{1... | collective-permute-start | bytes 798728 | tf_op jit(solution)/shard_map/ppermute | solution.py:383
  11.5 13.1 %collective-permute-start.4 = (bf16[1040,128]{1,0:T(8,128)(2,1)S(1)}, bf16[1040,128]{1,0:T(8,128)(2,1)S(1)}, u32[]{:S(2)}, u32[]{:S(2)}) collective-permute-start(bf16[1040,128]{1,0:T(8,128)(2,1)S(1)} %get-tuple-element.13.refs_0_), channel_id=1, source_target_pairs={{0,16},{16,32},{32,48},{48,64},{64,80},{80,96},{96,112},{112,0},{1... | collective-permute-start | bytes 798728 | tf_op jit(solution)/shard_map/ppermute | solution.py:380
  17.2 33.4 %collective-permute-start = (bf16[2,128,1792]{2,1,0:T(8,128)(2,1)}, bf16[2,128,1792]{2,1,0:T(8,128)(2,1)}, u32[]{:S(2)}, u32[]{:S(2)}) collective-permute-start(bf16[2,128,1792]{2,1,0:T(8,128)(2,1)} %get-tuple-element.11), channel_id=1, source_target_pairs={{0,136},{8,128},{128,8},{136,0},{1,137},{9,129},{129,9},{137,1},{2... | collective-permute-start | bytes 2752520 | tf_op jit(solution)/shard_map/ppermute | solution.py:373
  18.6 8.8 %collective-permute-start.10 = (bf16[1040,128]{1,0:T(8,128)(2,1)S(1)}, bf16[1040,128]{1,0:T(8,128)(2,1)S(1)}, u32[]{:S(2)}, u32[]{:S(2)}) collective-permute-start(bf16[1040,128]{1,0:T(8,128)(2,1)S(1)} %collective-permute-done.2.window_in.refs_8_), channel_id=1, source_target_pairs={{0,112},{16,0},{32,16},{48,32},{64,48},{80,64},{96,80},{112,96},{1... | collective-permute-start | bytes 798728 | tf_op jit(solution)/shard_map/ppermute | solution.py:381
  21.9 14.8 %collective-permute-start.11 = (bf16[1040,128]{1,0:T(8,128)(2,1)S(1)}, bf16[1040,128]{1,0:T(8,128)(2,1)S(1)}, u32[]{:S(2)}, u32[]{:S(2)}) collective-permute-start(bf16[1040,128]{1,0:T(8,128)(2,1)S(1)} %collective-permute-done.2.window_in.refs_8_), channel_id=1, source_target_pairs={{0,16},{16,32},{32,48},{48,64},{64,80},{80,96},{96,112},{112,0},{1... | collective-permute-start | bytes 798728 | tf_op jit(solution)/shard_map/ppermute | solution.py:384
  22.0 11.1 %collective-permute-start.5 = (bf16[1040,128]{1,0:T(8,128)(2,1)S(1)}, bf16[1040,128]{1,0:T(8,128)(2,1)S(1)}, u32[]{:S(2)}, u32[]{:S(2)}) collective-permute-start(bf16[1040,128]{1,0:T(8,128)(2,1)S(1)} %collective-permute-done.3.refs_1_), channel_id=1, source_target_pairs={{0,112},{16,0},{32,16},{48,32},{64,48},{80,64},{96,80},{112,96},{1... | collective-permute-start | bytes 798728 | tf_op jit(solution)/shard_map/ppermute | solution.py:383
  24.7 12.1 %collective-permute-start.6 = (bf16[1040,128]{1,0:T(8,128)(2,1)S(1)}, bf16[1040,128]{1,0:T(8,128)(2,1)S(1)}, u32[]{:S(2)}, u32[]{:S(2)}) collective-permute-start(bf16[1040,128]{1,0:T(8,128)(2,1)S(1)} %collective-permute-done.4.refs_2_), channel_id=1, source_target_pairs={{0,16},{16,32},{32,48},{48,64},{64,80},{80,96},{96,112},{112,0},{1... | collective-permute-start | bytes 798728 | tf_op jit(solution)/shard_map/ppermute | solution.py:380
  27.4 11.4 %collective-permute-start.12 = (bf16[1040,128]{1,0:T(8,128)(2,1)S(1)}, bf16[1040,128]{1,0:T(8,128)(2,1)S(1)}, u32[]{:S(2)}, u32[]{:S(2)}) collective-permute-start(bf16[1040,128]{1,0:T(8,128)(2,1)S(1)} %collective-permute-done.10.refs_9_), channel_id=1, source_target_pairs={{0,112},{16,0},{32,16},{48,32},{64,48},{80,64},{96,80},{112,96},{1... | collective-permute-start | bytes 798728 | tf_op jit(solution)/shard_map/ppermute | solution.py:381
  33.1 40.7 %copy-start.5 = (bf16[1040,128]{1,0:T(8,128)(2,1)}, bf16[1040,128]{1,0:T(8,128)(2,1)S(1)}, u32[]{:S(2)}) copy-start(bf16[1040,128]{1,0:T(8,128)(2,1)S(1)} %collective-permute-done.5.refs_3_) | copy-start | bytes 798724
  33.1 9.3 %collective-permute-start.18 = (bf16[1040,128]{1,0:T(8,128)(2,1)S(1)}, bf16[1040,128]{1,0:T(8,128)(2,1)}, u32[]{:S(2)}, u32[]{:S(2)}) collective-permute-start(bf16[1040,128]{1,0:T(8,128)(2,1)S(1)} %collective-permute-done.2.window_in.refs_8_), channel_id=1, source_target_pairs={{0,8},{8,0},{1,9},{9,1},{2,10},{10,2},{3,11},{11,3},{4,12},{12,4},... | collective-permute-start | bytes 798728 | tf_op jit(solution)/shard_map/ppermute | solution.py:376
  36.8 37.1 %copy-start.7 = (bf16[1040,128]{1,0:T(8,128)(2,1)}, bf16[1040,128]{1,0:T(8,128)(2,1)S(1)}, u32[]{:S(2)}) copy-start(bf16[1040,128]{1,0:T(8,128)(2,1)S(1)} %collective-permute-done.6.refs_4_) | copy-start | bytes 798724
  36.8 8.1 %collective-permute-start.8 = (bf16[1040,128]{1,0:T(8,128)(2,1)S(1)}, bf16[1040,128]{1,0:T(8,128)(2,1)S(1)}, u32[]{:S(2)}, u32[]{:S(2)}) collective-permute-start(bf16[1040,128]{1,0:T(8,128)(2,1)S(1)} %collective-permute-done.6.refs_4_), channel_id=1, source_target_pairs={{0,16},{16,32},{32,48},{48,64},{64,80},{80,96},{96,112},{112,0},{1... | collective-permute-start | bytes 798728 | tf_op jit(solution)/shard_map/ppermute | solution.py:380
  36.8 37.1 %copy-start.4 = (bf16[1040,128]{1,0:T(8,128)(2,1)}, bf16[1040,128]{1,0:T(8,128)(2,1)S(1)}, u32[]{:S(2)}) copy-start(bf16[1040,128]{1,0:T(8,128)(2,1)S(1)} %collective-permute-done.11.refs_10_) | copy-start | bytes 798724
  36.8 13.8 %collective-permute-start.13 = (bf16[1040,128]{1,0:T(8,128)(2,1)S(1)}, bf16[1040,128]{1,0:T(8,128)(2,1)S(1)}, u32[]{:S(2)}, u32[]{:S(2)}) collective-permute-start(bf16[1040,128]{1,0:T(8,128)(2,1)S(1)} %collective-permute-done.11.refs_10_), channel_id=1, source_target_pairs={{0,16},{16,32},{32,48},{48,64},{64,80},{80,96},{96,112},{112,0},{1... | collective-permute-start | bytes 798728 | tf_op jit(solution)/shard_map/ppermute | solution.py:384
  38.9 35.0 %copy-start.6 = (bf16[1040,128]{1,0:T(8,128)(2,1)}, bf16[1040,128]{1,0:T(8,128)(2,1)S(1)}, u32[]{:S(2)}) copy-start(bf16[1040,128]{1,0:T(8,128)(2,1)S(1)} %collective-permute-done.12.refs_11_) | copy-start | bytes 798724
  38.9 11.9 %collective-permute-start.14 = (bf16[1040,128]{1,0:T(8,128)(2,1)S(1)}, bf16[1040,128]{1,0:T(8,128)(2,1)S(1)}, u32[]{:S(2)}, u32[]{:S(2)}) collective-permute-start(bf16[1040,128]{1,0:T(8,128)(2,1)S(1)} %collective-permute-done.12.refs_11_), channel_id=1, source_target_pairs={{0,112},{16,0},{32,16},{48,32},{64,48},{80,64},{96,80},{112,96},{1... | collective-permute-start | bytes 798728 | tf_op jit(solution)/shard_map/ppermute | solution.py:381
  42.4 12.9 %collective-permute-start.17 = (bf16[2,128,2048]{2,1,0:T(8,128)(2,1)}, bf16[2,128,2048]{2,1,0:T(8,128)(2,1)}, u32[]{:S(2)}, u32[]{:S(2)}) collective-permute-start(bf16[2,128,2048]{2,1,0:T(8,128)(2,1)} %copy-done.12), channel_id=1, source_target_pairs={{0,8},{8,0},{1,9},{9,1},{2,10},{10,2},{3,11},{11,3},{4,12},{12,4},... | collective-permute-start | bytes 3145736 | tf_op jit(solution)/shard_map/ppermute | solution.py:374
  44.9 29.0 %copy-start.8 = (bf16[1040,128]{1,0:T(8,128)(2,1)}, bf16[1040,128]{1,0:T(8,128)(2,1)S(1)}, u32[]{:S(2)}) copy-start(bf16[1040,128]{1,0:T(8,128)(2,1)S(1)} %collective-permute-done.8.refs_6_) | copy-start | bytes 798724
  44.9 8.5 %collective-permute-start.7 = (bf16[1040,128]{1,0:T(8,128)(2,1)S(1)}, bf16[1040,128]{1,0:T(8,128)(2,1)}, u32[]{:S(2)}, u32[]{:S(2)}) collective-permute-start(bf16[1040,128]{1,0:T(8,128)(2,1)S(1)} %collective-permute-done.5.refs_3_), channel_id=1, source_target_pairs={{0,112},{16,0},{32,16},{48,32},{64,48},{80,64},{96,80},{112,96},{1... | collective-permute-start | bytes 798728 | tf_op jit(solution)/shard_map/ppermute | solution.py:383
  50.6 23.3 %copy-start.9 = (bf16[1040,128]{1,0:T(8,128)(2,1)}, bf16[1040,128]{1,0:T(8,128)(2,1)S(1)}, u32[]{:S(2)}) copy-start(bf16[1040,128]{1,0:T(8,128)(2,1)S(1)} %collective-permute-done.13.refs_12_) | copy-start | bytes 798724
  50.6 7.3 %collective-permute-start.9 = (bf16[1040,128]{1,0:T(8,128)(2,1)S(1)}, bf16[1040,128]{1,0:T(8,128)(2,1)}, u32[]{:S(2)}, u32[]{:S(2)}) collective-permute-start(bf16[1040,128]{1,0:T(8,128)(2,1)S(1)} %collective-permute-done.8.refs_6_), channel_id=1, source_target_pairs={{0,16},{16,32},{32,48},{48,64},{64,80},{80,96},{96,112},{112,0},{1... | collective-permute-start | bytes 798728 | tf_op jit(solution)/shard_map/ppermute | solution.py:380
  50.6 13.0 %collective-permute-start.15 = (bf16[1040,128]{1,0:T(8,128)(2,1)S(1)}, bf16[1040,128]{1,0:T(8,128)(2,1)}, u32[]{:S(2)}, u32[]{:S(2)}) collective-permute-start(bf16[1040,128]{1,0:T(8,128)(2,1)S(1)} %collective-permute-done.13.refs_12_), channel_id=1, source_target_pairs={{0,16},{16,32},{32,48},{48,64},{64,80},{80,96},{96,112},{112,0},{1... | collective-permute-start | bytes 798728 | tf_op jit(solution)/shard_map/ppermute | solution.py:384
  50.7 23.2 %copy-start.10 = (bf16[1040,128]{1,0:T(8,128)(2,1)}, bf16[1040,128]{1,0:T(8,128)(2,1)S(1)}, u32[]{:S(2)}) copy-start(bf16[1040,128]{1,0:T(8,128)(2,1)S(1)} %collective-permute-done.14.refs_13_) | copy-start | bytes 798724
  50.7 12.9 %collective-permute-start.16 = (bf16[1040,128]{1,0:T(8,128)(2,1)S(1)}, bf16[1040,128]{1,0:T(8,128)(2,1)}, u32[]{:S(2)}, u32[]{:S(2)}) collective-permute-start(bf16[1040,128]{1,0:T(8,128)(2,1)S(1)} %collective-permute-done.14.refs_13_), channel_id=1, source_target_pairs={{0,112},{16,0},{32,16},{48,32},{64,48},{80,64},{96,80},{112,96},{1... | collective-permute-start | bytes 798728 | tf_op jit(solution)/shard_map/ppermute | solution.py:381
  53.4 20.5 %collective-permute-start.1 = (bf16[2,128,1792]{2,1,0:T(8,128)(2,1)}, bf16[2,128,1792]{2,1,0:T(8,128)(2,1)S(1)}, u32[]{:S(2)}, u32[]{:S(2)}) collective-permute-start(bf16[2,128,1792]{2,1,0:T(8,128)(2,1)} %shard_map.65), channel_id=1, source_target_pairs={{0,128},{128,0},{1,129},{129,1},{2,130},{130,2},{3,131},{131,3},{4... | collective-permute-start | bytes 2752520 | tf_op jit(solution)/shard_map/ppermute | solution.py:375
  69.9 10.3 %collective-permute-start.19 = (f32[2,256,512]{2,1,0:T(8,128)}, f32[2,256,512]{2,1,0:T(8,128)S(1)}, u32[]{:S(2)}, u32[]{:S(2)}) collective-permute-start(f32[2,256,512]{2,1,0:T(8,128)} %shard_map.68), channel_id=1, source_target_pairs={{0,8},{8,0},{1,9},{9,1},{2,10},{10,2},{3,11},{11,3},{4,12},{12,4},... | collective-permute-start | bytes 3145736 | tf_op jit(solution)/shard_map/ppermute | solution.py:387
  83.1 16.4 %all-to-all-start = ((bf16[16,32,512]{2,1,0:T(8,128)(2,1)}), bf16[16,32,512]{2,1,0:T(8,128)(2,1)S(1)}, u32[]{:S(2)}, u32[]{:S(2)}) async-start(bf16[16,32,512]{2,1,0:T(8,128)(2,1)} %shard_map.69), calls=%async_computation | async-start | bytes 1048576 | tf_op jit(solution)/shard_map/all_to_all | solution.py:414
  90.6 25.5 %copy-start.15 = (s32[8]{0:T(128)S(1)}, s32[8]{0:T(128)}, u32[]{:S(2)}) copy-start(s32[8]{0:T(128)} %constant.128) | copy-start | bytes 100
  105.0 41.1 %all-to-all-start.1 = ((bf16[256,16,128]{2,1,0:T(8,128)(2,1)}), bf16[256,16,128]{2,1,0:T(8,128)(2,1)S(1)}, u32[]{:S(2)}, u32[]{:S(2)}) async-start(bf16[256,16,128]{2,1,0:T(8,128)(2,1)} %bitcast.6), calls=%async_computation.1 | async-start | bytes 2097152 | tf_op jit(solution)/shard_map/all_to_all | solution.py:417
  123.8 3.3 %collective-permute-start.20 = (bf16[16,128]{1,0:T(8,128)(2,1)S(1)}, bf16[16,128]{1,0:T(8,128)(2,1)S(1)}, u32[]{:S(2)}, u32[]{:S(2)}) collective-permute-start(bf16[16,128]{1,0:T(8,128)(2,1)S(1)} %concatenate.15), channel_id=1, source_target_pairs={{0,8},{8,0},{1,9},{9,1},{2,10},{10,2},{3,11},{11,3},{4,12},{12,4},... | collective-permute-start | bytes 12296 | tf_op jit(solution)/shard_map/ppermute | solution.py:395
  (8 other events, 51.0 us)

commit v4 on v3

--- a/solution.py
+++ b/solution.py
@@ -212,12 +212,12 @@
             elif n < count - 1:
                 total[...] += value
             else:
-                out[0] = total[:size] + value[:size]
-                out[1] = total[size:] + value[size:]
+                out[0] = (total[:size] + value[:size]).astype(out.dtype)
+                out[1] = (total[size:] + value[size:]).astype(out.dtype)
 
     return pl.pallas_call(
         kernel,
-        out_shape=jax.ShapeDtypeStruct((2, size, WINDOW), F32),
+        out_shape=jax.ShapeDtypeStruct((2, size, WINDOW), BF if line is None else F32),
         in_specs=[SMEM, HBM if line is None else ANY] + [ANY] * (2 + 2 * count),
         scratch_shapes=[
             pltpu.VMEM((2 * size, WINDOW), F32),
@@ -250,8 +250,8 @@
         where = xl if block == 0 else 1 - xl
         order = order_own[...] if block == 0 else order_other[...]
         rows = slice(block * SHOTS, (block + 1) * SHOTS)
-        real = keep[0, rows] + came[0, rows]
-        imag = keep[1, rows] + came[1, rows]
+        real = keep[0, rows].astype(F32) + came[0, rows]
+        imag = keep[1, rows].astype(F32) + came[1, rows]
         er = (real * wr - imag * wi).astype(BF)
         ei = (real * wi + imag * wr).astype(BF)
         sr = dot(order, er).astype(BF)

time: 148 us -> 146 us (0.986)
    unnamed x34 -> x32, local copies, waits for them, and re-layouts: 6.6 us -> 5.36 us
  transfers between devices with their start and end apart: 23 -> 23, of which waited for: 12 -> 12; matrix products, arithmetic and copies ran while one was open for 8% -> 8% of each run, Pallas kernels for 11% -> 10%
where the time goes in v4:
time: 146 us
  starting transfers between devices  51.9 us (36%)
  waiting for transfers between devices  51.2 us (35%)
  Pallas kernels  23.8 us (16%)
  local copies, waits for them, and re-layouts  14 us (10%)
  other arithmetic  4.38 us (3%)
    all_to_all x1, waiting for transfers between devices, shards(): arrived = lax.all_to_all(rows, SHOT_AXES + FREQ_AXES, 0, 0, tiled=True)  17.8 us
    ppermute x4, starting transfers between devices, shards(): far[-step] = lax.ppermute(far[1 - step], 'z', left)  12.4 us
    pallas_call x2, Pallas kernels, product(): pl.pallas_call(kernel, out_shape=jax.ShapeDtypeStruct((2, size, WINDOW),...  11.4 us
    ppermute x3, waiting for transfers between devices, shards(): far[step] = lax.ppermute(far[step - 1], 'z', right)  10.8 us
    all_to_all x1, starting transfers between devices, shards(): arrived = lax.all_to_all(rows, SHOT_AXES + FREQ_AXES, 0, 0, tiled=True)  10.3 us
    ppermute x3, starting transfers between devices, shards(): near[-step] = lax.ppermute(near[1 - step], 'z', left)  8.88 us
    all_to_all x1, waiting for transfers between devices, shards(): spectra = lax.all_to_all(estimate, FREQ_AXES + ('xl',), 0, 0, tiled=True)  8.16 us
    all_to_all x1, starting transfers between devices, shards(): spectra = lax.all_to_all(estimate, FREQ_AXES + ('xl',), 0, 0, tiled=True)  7.42 us
  transfers between devices with their start and end apart: 23, of which 12 were waited for; matrix products, arithmetic and copies ran while one was open for 8% of the time, Pallas kernels for 10%

profile of v4, /device:TPU:1, one launch (start us, length us, event | category | flops | bytes accessed | tf_op | source)
XLA Modules:
  0.0 145.6 jit_solution(4149663074764943931)
XLA Ops:
  0.7 2.2 %copy-done = bf16[2,2,128,4096]{3,2,1,0:T(8,128)(2,1)S(1)} copy-done((bf16[2,2,128,4096]{3,2,1,0:T(8,128)(2,1)S(1)}, bf16[2,2,128,4096]{3,2,1,0:T(8,128)(2,1)}, u32[]{:S(2)}) %copy-start) | copy-done | bytes 4194328
  3.8 2.1 %collective-permute-start.2 = (bf16[1040,128]{1,0:T(8,128)(2,1)S(1)}, bf16[1040,128]{1,0:T(8,128)(2,1)S(1)}, u32[]{:S(2)}, u32[]{:S(2)}) collective-permute-start(bf16[1040,128]{1,0:T(8,128)(2,1)S(1)} %get-tuple-element.12), channel_id=1, source_target_pairs={{0,128},{128,0},{1,129},{129,1},{2,130},{130,2},{3,131},{131,3},{4... | collective-permute-start | bytes 798728 | tf_op jit(solution)/shard_map/ppermute | solution.py:371
  6.0 5.6 %collective-permute-start.3 = (bf16[1040,128]{1,0:T(8,128)(2,1)S(1)}, bf16[1040,128]{1,0:T(8,128)(2,1)S(1)}, u32[]{:S(2)}, u32[]{:S(2)}) collective-permute-start(bf16[1040,128]{1,0:T(8,128)(2,1)S(1)} %get-tuple-element.13.refs_0_), channel_id=1, source_target_pairs={{0,112},{16,0},{32,16},{48,32},{64,48},{80,64},{96,80},{112,96},{1... | collective-permute-start | bytes 798728 | tf_op jit(solution)/shard_map/ppermute | solution.py:383
  11.5 3.8 %shard_map.64 = (bf16[2,128,1792]{2,1,0:T(8,128)(2,1)}, bf16[2,128,1792]{2,1,0:T(8,128)(2,1)S(1)}, bf16[2,128,2048]{2,1,0:T(8,128)(2,1)S(1)}) custom-call(s32[3]{0:T(128)S(1)} %pad_add_fusion.place, bf16[2,2,128,4096]{3,2,1,0:T(8,128)(2,1)} %line_in.1), custom_call_target="tpu_custom_call" | custom-call | tf_op jit(solution)/shard_map/pallas_call | solution.py:111
  17.2 1.4 collective-permute-start
  18.6 3.0 %collective-permute-start.10 = (bf16[1040,128]{1,0:T(8,128)(2,1)S(1)}, bf16[1040,128]{1,0:T(8,128)(2,1)S(1)}, u32[]{:S(2)}, u32[]{:S(2)}) collective-permute-start(bf16[1040,128]{1,0:T(8,128)(2,1)S(1)} %collective-permute-done.2.window_in.refs_8_), channel_id=1, source_target_pairs={{0,112},{16,0},{32,16},{48,32},{64,48},{80,64},{96,80},{112,96},{1... | collective-permute-start | bytes 798728 | tf_op jit(solution)/shard_map/ppermute | solution.py:381
  22.0 2.7 %collective-permute-start.5 = (bf16[1040,128]{1,0:T(8,128)(2,1)S(1)}, bf16[1040,128]{1,0:T(8,128)(2,1)S(1)}, u32[]{:S(2)}, u32[]{:S(2)}) collective-permute-start(bf16[1040,128]{1,0:T(8,128)(2,1)S(1)} %collective-permute-done.3.refs_1_), channel_id=1, source_target_pairs={{0,112},{16,0},{32,16},{48,32},{64,48},{80,64},{96,80},{112,96},{1... | collective-permute-start | bytes 798728 | tf_op jit(solution)/shard_map/ppermute | solution.py:383
  24.7 2.8 %collective-permute-done.10.refs_9_ = bf16[1040,128]{1,0:T(8,128)(2,1)S(1)} collective-permute-done((bf16[1040,128]{1,0:T(8,128)(2,1)S(1)}, bf16[1040,128]{1,0:T(8,128)(2,1)S(1)}, u32[]{:S(2)}, u32[]{:S(2)}) %collective-permute-start.10) | collective-permute-done | bytes 266272 | tf_op jit(solution)/shard_map/ppermute | solution.py:381
  27.4 3.4 %collective-permute-start.12 = (bf16[1040,128]{1,0:T(8,128)(2,1)S(1)}, bf16[1040,128]{1,0:T(8,128)(2,1)S(1)}, u32[]{:S(2)}, u32[]{:S(2)}) collective-permute-start(bf16[1040,128]{1,0:T(8,128)(2,1)S(1)} %collective-permute-done.10.refs_9_), channel_id=1, source_target_pairs={{0,112},{16,0},{32,16},{48,32},{64,48},{80,64},{96,80},{112,96},{1... | collective-permute-start | bytes 798728 | tf_op jit(solution)/shard_map/ppermute | solution.py:381
  30.9 2.2 %collective-permute-done.5.refs_3_ = bf16[1040,128]{1,0:T(8,128)(2,1)S(1)} collective-permute-done((bf16[1040,128]{1,0:T(8,128)(2,1)S(1)}, bf16[1040,128]{1,0:T(8,128)(2,1)S(1)}, u32[]{:S(2)}, u32[]{:S(2)}) %collective-permute-start.5) | collective-permute-done | bytes 266272 | tf_op jit(solution)/shard_map/ppermute | solution.py:383
  34.2 2.6 %collective-permute-done.6.refs_4_ = bf16[1040,128]{1,0:T(8,128)(2,1)S(1)} collective-permute-done((bf16[1040,128]{1,0:T(8,128)(2,1)S(1)}, bf16[1040,128]{1,0:T(8,128)(2,1)S(1)}, u32[]{:S(2)}, u32[]{:S(2)}) %collective-permute-start.6) | collective-permute-done | bytes 266272 | tf_op jit(solution)/shard_map/ppermute | solution.py:380
  36.9 2.0 %collective-permute-done.12.refs_11_ = bf16[1040,128]{1,0:T(8,128)(2,1)S(1)} collective-permute-done((bf16[1040,128]{1,0:T(8,128)(2,1)S(1)}, bf16[1040,128]{1,0:T(8,128)(2,1)S(1)}, u32[]{:S(2)}, u32[]{:S(2)}) %collective-permute-start.12) | collective-permute-done | bytes 266272 | tf_op jit(solution)/shard_map/ppermute | solution.py:381
  38.9 3.4 %collective-permute-start.14 = (bf16[1040,128]{1,0:T(8,128)(2,1)S(1)}, bf16[1040,128]{1,0:T(8,128)(2,1)S(1)}, u32[]{:S(2)}, u32[]{:S(2)}) collective-permute-start(bf16[1040,128]{1,0:T(8,128)(2,1)S(1)} %collective-permute-done.12.refs_11_), channel_id=1, source_target_pairs={{0,112},{16,0},{32,16},{48,32},{64,48},{80,64},{96,80},{112,96},{1... | collective-permute-start | bytes 798728 | tf_op jit(solution)/shard_map/ppermute | solution.py:381
  42.4 1.1 collective-permute-start.17
  43.5 1.4 collective-permute-done.8.refs_6_
  45.6 5.1 %collective-permute-done.13.refs_12_ = bf16[1040,128]{1,0:T(8,128)(2,1)S(1)} collective-permute-done((bf16[1040,128]{1,0:T(8,128)(2,1)S(1)}, bf16[1040,128]{1,0:T(8,128)(2,1)S(1)}, u32[]{:S(2)}, u32[]{:S(2)}) %collective-permute-start.13) | collective-permute-done | bytes 266272 | tf_op jit(solution)/shard_map/ppermute | solution.py:384
  50.7 2.7 %collective-permute-start.16 = (bf16[1040,128]{1,0:T(8,128)(2,1)S(1)}, bf16[1040,128]{1,0:T(8,128)(2,1)}, u32[]{:S(2)}, u32[]{:S(2)}) collective-permute-start(bf16[1040,128]{1,0:T(8,128)(2,1)S(1)} %collective-permute-done.14.refs_13_), channel_id=1, source_target_pairs={{0,112},{16,0},{32,16},{48,32},{64,48},{80,64},{96,80},{112,96},{1... | collective-permute-start | bytes 798728 | tf_op jit(solution)/shard_map/ppermute | solution.py:381
  53.4 1.9 %collective-permute-start.1 = (bf16[2,128,1792]{2,1,0:T(8,128)(2,1)}, bf16[2,128,1792]{2,1,0:T(8,128)(2,1)S(1)}, u32[]{:S(2)}, u32[]{:S(2)}) collective-permute-start(bf16[2,128,1792]{2,1,0:T(8,128)(2,1)} %shard_map.65), channel_id=1, source_target_pairs={{0,128},{128,0},{1,129},{129,1},{2,130},{130,2},{3,131},{131,3},{4... | collective-permute-start | bytes 2752520 | tf_op jit(solution)/shard_map/ppermute | solution.py:375
  55.3 2.7 %collective-permute-done.9.refs_7_ = bf16[1040,128]{1,0:T(8,128)(2,1)} collective-permute-done((bf16[1040,128]{1,0:T(8,128)(2,1)S(1)}, bf16[1040,128]{1,0:T(8,128)(2,1)}, u32[]{:S(2)}, u32[]{:S(2)}) %collective-permute-start.9) | collective-permute-done | bytes 266272 | tf_op jit(solution)/shard_map/ppermute | solution.py:380
  58.0 5.7 %collective-permute-done.15.refs_14_ = bf16[1040,128]{1,0:T(8,128)(2,1)} collective-permute-done((bf16[1040,128]{1,0:T(8,128)(2,1)S(1)}, bf16[1040,128]{1,0:T(8,128)(2,1)}, u32[]{:S(2)}, u32[]{:S(2)}) %collective-permute-start.15) | collective-permute-done | bytes 266272 | tf_op jit(solution)/shard_map/ppermute | solution.py:384
  63.7 6.2 %shard_map.68 = f32[2,256,512]{2,1,0:T(8,128)} custom-call(s32[3]{0:T(128)S(1)} %pad_add_fusion.place, bf16[2,128,2048]{2,1,0:T(8,128)(2,1)} %collective-permute-done.17.line_in, bf16[2,128,1792]{2,1,0:T(8,128)(2,1)} %collective-permute-done.earlier.rest_in, bf16[1040,128]{1,0:T(8,128)(2,1)} %collective-permute-done.18.window_in, ...), custom_call_target="tpu_custom_call" | custom-call | flops 2147483648 | bytes 4194304 | tf_op jit(solution)/shard_map/pallas_call | solution.py:218
  69.9 2.9 %collective-permute-start.19 = (f32[2,256,512]{2,1,0:T(8,128)}, f32[2,256,512]{2,1,0:T(8,128)S(1)}, u32[]{:S(2)}, u32[]{:S(2)}) collective-permute-start(f32[2,256,512]{2,1,0:T(8,128)} %shard_map.68), channel_id=1, source_target_pairs={{0,8},{8,0},{1,9},{9,1},{2,10},{10,2},{3,11},{11,3},{4,12},{12,4},... | collective-permute-start | bytes 3145736 | tf_op jit(solution)/shard_map/ppermute | solution.py:387
  73.9 5.2 %shard_map.67.keep = bf16[2,256,512]{2,1,0:T(8,128)(2,1)S(1)} custom-call(s32[3]{0:T(128)S(1)} %pad_add_fusion.place, bf16[2,2,128,4096]{3,2,1,0:T(8,128)(2,1)} %line_in.1, bf16[2,128,1792]{2,1,0:T(8,128)(2,1)S(1)} %collective-permute-done.1.rest_in, bf16[1040,128]{1,0:T(8,128)(2,1)S(1)} %collective-permute-done.2.window_in.refs_8_, ...), custom_call_target="tpu_custom_call" | custom-call | flops 2147483648 | bytes 4194304 | tf_op jit(solution)/shard_map/pallas_call | solution.py:218
  79.2 1.7 %shard_map.69 = bf16[16,32,512]{2,1,0:T(8,128)(2,1)} custom-call(s32[3]{0:T(128)S(1)} %pad_add_fusion.place, f32[2,2]{1,0:T(2,128)S(1)} %copy-done.10, bf16[2,256,512]{2,1,0:T(8,128)(2,1)S(1)} %shard_map.67.keep, f32[2,256,512]{2,1,0:T(8,128)S(1)} %collective-permute-done.19.came, bf16[128,128]{1,0:T(8,128)(2,1)S(1)} %get-tuple-element.22.order_own, ...), custom_call_target="tpu_custom_call" | custom-call | tf_op jit(solution)/shard_map/pallas_call | solution.py:266
  80.9 7.4 %all-to-all-start = ((bf16[16,32,512]{2,1,0:T(8,128)(2,1)}), bf16[16,32,512]{2,1,0:T(8,128)(2,1)S(1)}, u32[]{:S(2)}, u32[]{:S(2)}) async-start(bf16[16,32,512]{2,1,0:T(8,128)(2,1)} %shard_map.69), calls=%async_computation | async-start | bytes 1048576 | tf_op jit(solution)/shard_map/all_to_all | solution.py:414
  89.2 8.2 %all-to-all-done.spectra = bf16[16,32,512]{2,1,0:T(8,128)(2,1)S(1)} async-done(((bf16[16,32,512]{2,1,0:T(8,128)(2,1)}), bf16[16,32,512]{2,1,0:T(8,128)(2,1)S(1)}, u32[]{:S(2)}, u32[]{:S(2)}) %all-to-all-start) | async-done | bytes 524320 | tf_op jit(solution)/shard_map/all_to_all | solution.py:414
  97.3 1.2 copy-done.1
  98.6 4.3 %shard_map.70 = bf16[128,2,16,128]{3,2,1,0:T(8,128)(2,1)} custom-call(bf16[16,32,512]{2,1,0:T(8,128)(2,1)S(1)} %all-to-all-done.spectra, bf16[1024,512]{1,0:T(8,128)(2,1)S(1)} %copy-done.1, s32[16,512]{1,0:T(8,128)S(1)} %select_reduce_fusion.trace_map, bf16[1024,512]{1,0:T(8,128)(2,1)S(1)} %get-tuple-element.23.spread, ...), custom_call_target="tpu_custom_call" | custom-call | tf_op jit(solution)/shard_map/pallas_call | solution.py:299
  102.9 10.3 %all-to-all-start.1 = ((bf16[256,16,128]{2,1,0:T(8,128)(2,1)}), bf16[256,16,128]{2,1,0:T(8,128)(2,1)S(1)}, u32[]{:S(2)}, u32[]{:S(2)}) async-start(bf16[256,16,128]{2,1,0:T(8,128)(2,1)} %bitcast.6), calls=%async_computation.1 | async-start | bytes 2097152 | tf_op jit(solution)/shard_map/all_to_all | solution.py:417
  121.6 2.2 %collective-permute-start.20 = (bf16[16,128]{1,0:T(8,128)(2,1)S(1)}, bf16[16,128]{1,0:T(8,128)(2,1)S(1)}, u32[]{:S(2)}, u32[]{:S(2)}) collective-permute-start(bf16[16,128]{1,0:T(8,128)(2,1)S(1)} %concatenate.15), channel_id=1, source_target_pairs={{0,8},{8,0},{1,9},{9,1},{2,10},{10,2},{3,11},{11,3},{4,12},{12,4},... | collective-permute-start | bytes 12296 | tf_op jit(solution)/shard_map/ppermute | solution.py:395
  126.2 17.8 %all-to-all-done.1.arrived = bf16[256,16,128]{2,1,0:T(8,128)(2,1)S(1)} async-done(((bf16[256,16,128]{2,1,0:T(8,128)(2,1)}), bf16[256,16,128]{2,1,0:T(8,128)(2,1)S(1)}, u32[]{:S(2)}, u32[]{:S(2)}) %all-to-all-start.1) | async-done | bytes 1048608 | tf_op jit(solution)/shard_map/all_to_all | solution.py:417
  144.0 1.7 %shard_map.71 = bf16[4,256,512]{2,1,0:T(8,128)(2,1)} custom-call(bf16[256,16,128]{2,1,0:T(8,128)(2,1)S(1)} %all-to-all-done.1.arrived, bf16[16,256,256]{2,1,0:T(8,128)(2,1)S(1)} %fusion.turns), custom_call_target="tpu_custom_call" | custom-call | tf_op jit(solution)/shard_map/pallas_call | solution.py:320
  (107 shorter events, 18.7 us)
Async XLA Ops:
  3.8 70.0 %copy-start.2 = (bf16[1040,128]{1,0:T(8,128)(2,1)}, bf16[1040,128]{1,0:T(8,128)(2,1)S(1)}, u32[]{:S(2)}) copy-start(bf16[1040,128]{1,0:T(8,128)(2,1)S(1)} %get-tuple-element.13.refs_0_) | copy-start | bytes 798724
  3.8 14.8 %collective-permute-start.2 = (bf16[1040,128]{1,0:T(8,128)(2,1)S(1)}, bf16[1040,128]{1,0:T(8,128)(2,1)S(1)}, u32[]{:S(2)}, u32[]{:S(2)}) collective-permute-start(bf16[1040,128]{1,0:T(8,128)(2,1)S(1)} %get-tuple-element.12), channel_id=1, source_target_pairs={{0,128},{128,0},{1,129},{129,1},{2,130},{130,2},{3,131},{131,3},{4... | collective-permute-start | bytes 798728 | tf_op jit(solution)/shard_map/ppermute | solution.py:371
  6.0 16.0 %collective-permute-start.3 = (bf16[1040,128]{1,0:T(8,128)(2,1)S(1)}, bf16[1040,128]{1,0:T(8,128)(2,1)S(1)}, u32[]{:S(2)}, u32[]{:S(2)}) collective-permute-start(bf16[1040,128]{1,0:T(8,128)(2,1)S(1)} %get-tuple-element.13.refs_0_), channel_id=1, source_target_pairs={{0,112},{16,0},{32,16},{48,32},{64,48},{80,64},{96,80},{112,96},{1... | collective-permute-start | bytes 798728 | tf_op jit(solution)/shard_map/ppermute | solution.py:383
  11.5 13.1 %collective-permute-start.4 = (bf16[1040,128]{1,0:T(8,128)(2,1)S(1)}, bf16[1040,128]{1,0:T(8,128)(2,1)S(1)}, u32[]{:S(2)}, u32[]{:S(2)}) collective-permute-start(bf16[1040,128]{1,0:T(8,128)(2,1)S(1)} %get-tuple-element.13.refs_0_), channel_id=1, source_target_pairs={{0,16},{16,32},{32,48},{48,64},{64,80},{80,96},{96,112},{112,0},{1... | collective-permute-start | bytes 798728 | tf_op jit(solution)/shard_map/ppermute | solution.py:380
  17.2 33.4 %collective-permute-start = (bf16[2,128,1792]{2,1,0:T(8,128)(2,1)}, bf16[2,128,1792]{2,1,0:T(8,128)(2,1)}, u32[]{:S(2)}, u32[]{:S(2)}) collective-permute-start(bf16[2,128,1792]{2,1,0:T(8,128)(2,1)} %get-tuple-element.11), channel_id=1, source_target_pairs={{0,136},{8,128},{128,8},{136,0},{1,137},{9,129},{129,9},{137,1},{2... | collective-permute-start | bytes 2752520 | tf_op jit(solution)/shard_map/ppermute | solution.py:373
  18.6 8.8 %collective-permute-start.10 = (bf16[1040,128]{1,0:T(8,128)(2,1)S(1)}, bf16[1040,128]{1,0:T(8,128)(2,1)S(1)}, u32[]{:S(2)}, u32[]{:S(2)}) collective-permute-start(bf16[1040,128]{1,0:T(8,128)(2,1)S(1)} %collective-permute-done.2.window_in.refs_8_), channel_id=1, source_target_pairs={{0,112},{16,0},{32,16},{48,32},{64,48},{80,64},{96,80},{112,96},{1... | collective-permute-start | bytes 798728 | tf_op jit(solution)/shard_map/ppermute | solution.py:381
  21.9 14.8 %collective-permute-start.11 = (bf16[1040,128]{1,0:T(8,128)(2,1)S(1)}, bf16[1040,128]{1,0:T(8,128)(2,1)S(1)}, u32[]{:S(2)}, u32[]{:S(2)}) collective-permute-start(bf16[1040,128]{1,0:T(8,128)(2,1)S(1)} %collective-permute-done.2.window_in.refs_8_), channel_id=1, source_target_pairs={{0,16},{16,32},{32,48},{48,64},{64,80},{80,96},{96,112},{112,0},{1... | collective-permute-start | bytes 798728 | tf_op jit(solution)/shard_map/ppermute | solution.py:384
  22.0 11.1 %collective-permute-start.5 = (bf16[1040,128]{1,0:T(8,128)(2,1)S(1)}, bf16[1040,128]{1,0:T(8,128)(2,1)S(1)}, u32[]{:S(2)}, u32[]{:S(2)}) collective-permute-start(bf16[1040,128]{1,0:T(8,128)(2,1)S(1)} %collective-permute-done.3.refs_1_), channel_id=1, source_target_pairs={{0,112},{16,0},{32,16},{48,32},{64,48},{80,64},{96,80},{112,96},{1... | collective-permute-start | bytes 798728 | tf_op jit(solution)/shard_map/ppermute | solution.py:383
  24.7 12.1 %collective-permute-start.6 = (bf16[1040,128]{1,0:T(8,128)(2,1)S(1)}, bf16[1040,128]{1,0:T(8,128)(2,1)S(1)}, u32[]{:S(2)}, u32[]{:S(2)}) collective-permute-start(bf16[1040,128]{1,0:T(8,128)(2,1)S(1)} %collective-permute-done.4.refs_2_), channel_id=1, source_target_pairs={{0,16},{16,32},{32,48},{48,64},{64,80},{80,96},{96,112},{112,0},{1... | collective-permute-start | bytes 798728 | tf_op jit(solution)/shard_map/ppermute | solution.py:380
  27.4 11.4 %collective-permute-start.12 = (bf16[1040,128]{1,0:T(8,128)(2,1)S(1)}, bf16[1040,128]{1,0:T(8,128)(2,1)S(1)}, u32[]{:S(2)}, u32[]{:S(2)}) collective-permute-start(bf16[1040,128]{1,0:T(8,128)(2,1)S(1)} %collective-permute-done.10.refs_9_), channel_id=1, source_target_pairs={{0,112},{16,0},{32,16},{48,32},{64,48},{80,64},{96,80},{112,96},{1... | collective-permute-start | bytes 798728 | tf_op jit(solution)/shard_map/ppermute | solution.py:381
  33.1 40.7 %copy-start.4 = (bf16[1040,128]{1,0:T(8,128)(2,1)}, bf16[1040,128]{1,0:T(8,128)(2,1)S(1)}, u32[]{:S(2)}) copy-start(bf16[1040,128]{1,0:T(8,128)(2,1)S(1)} %collective-permute-done.5.refs_3_) | copy-start | bytes 798724
  33.1 9.3 %collective-permute-start.18 = (bf16[1040,128]{1,0:T(8,128)(2,1)S(1)}, bf16[1040,128]{1,0:T(8,128)(2,1)}, u32[]{:S(2)}, u32[]{:S(2)}) collective-permute-start(bf16[1040,128]{1,0:T(8,128)(2,1)S(1)} %collective-permute-done.2.window_in.refs_8_), channel_id=1, source_target_pairs={{0,8},{8,0},{1,9},{9,1},{2,10},{10,2},{3,11},{11,3},{4,12},{12,4},... | collective-permute-start | bytes 798728 | tf_op jit(solution)/shard_map/ppermute | solution.py:376
  36.8 37.1 %copy-start.6 = (bf16[1040,128]{1,0:T(8,128)(2,1)}, bf16[1040,128]{1,0:T(8,128)(2,1)S(1)}, u32[]{:S(2)}) copy-start(bf16[1040,128]{1,0:T(8,128)(2,1)S(1)} %collective-permute-done.6.refs_4_) | copy-start | bytes 798724
  36.8 8.1 %collective-permute-start.8 = (bf16[1040,128]{1,0:T(8,128)(2,1)S(1)}, bf16[1040,128]{1,0:T(8,128)(2,1)S(1)}, u32[]{:S(2)}, u32[]{:S(2)}) collective-permute-start(bf16[1040,128]{1,0:T(8,128)(2,1)S(1)} %collective-permute-done.6.refs_4_), channel_id=1, source_target_pairs={{0,16},{16,32},{32,48},{48,64},{64,80},{80,96},{96,112},{112,0},{1... | collective-permute-start | bytes 798728 | tf_op jit(solution)/shard_map/ppermute | solution.py:380
  36.8 37.1 %copy-start.3 = (bf16[1040,128]{1,0:T(8,128)(2,1)}, bf16[1040,128]{1,0:T(8,128)(2,1)S(1)}, u32[]{:S(2)}) copy-start(bf16[1040,128]{1,0:T(8,128)(2,1)S(1)} %collective-permute-done.11.refs_10_) | copy-start | bytes 798724
  36.8 13.8 %collective-permute-start.13 = (bf16[1040,128]{1,0:T(8,128)(2,1)S(1)}, bf16[1040,128]{1,0:T(8,128)(2,1)S(1)}, u32[]{:S(2)}, u32[]{:S(2)}) collective-permute-start(bf16[1040,128]{1,0:T(8,128)(2,1)S(1)} %collective-permute-done.11.refs_10_), channel_id=1, source_target_pairs={{0,16},{16,32},{32,48},{48,64},{64,80},{80,96},{96,112},{112,0},{1... | collective-permute-start | bytes 798728 | tf_op jit(solution)/shard_map/ppermute | solution.py:384
  38.8 35.0 %copy-start.5 = (bf16[1040,128]{1,0:T(8,128)(2,1)}, bf16[1040,128]{1,0:T(8,128)(2,1)S(1)}, u32[]{:S(2)}) copy-start(bf16[1040,128]{1,0:T(8,128)(2,1)S(1)} %collective-permute-done.12.refs_11_) | copy-start | bytes 798724
  38.9 11.9 %collective-permute-start.14 = (bf16[1040,128]{1,0:T(8,128)(2,1)S(1)}, bf16[1040,128]{1,0:T(8,128)(2,1)S(1)}, u32[]{:S(2)}, u32[]{:S(2)}) collective-permute-start(bf16[1040,128]{1,0:T(8,128)(2,1)S(1)} %collective-permute-done.12.refs_11_), channel_id=1, source_target_pairs={{0,112},{16,0},{32,16},{48,32},{64,48},{80,64},{96,80},{112,96},{1... | collective-permute-start | bytes 798728 | tf_op jit(solution)/shard_map/ppermute | solution.py:381
  42.4 12.9 %collective-permute-start.17 = (bf16[2,128,2048]{2,1,0:T(8,128)(2,1)}, bf16[2,128,2048]{2,1,0:T(8,128)(2,1)}, u32[]{:S(2)}, u32[]{:S(2)}) collective-permute-start(bf16[2,128,2048]{2,1,0:T(8,128)(2,1)} %copy-done.11), channel_id=1, source_target_pairs={{0,8},{8,0},{1,9},{9,1},{2,10},{10,2},{3,11},{11,3},{4,12},{12,4},... | collective-permute-start | bytes 3145736 | tf_op jit(solution)/shard_map/ppermute | solution.py:374
  44.9 29.0 %copy-start.7 = (bf16[1040,128]{1,0:T(8,128)(2,1)}, bf16[1040,128]{1,0:T(8,128)(2,1)S(1)}, u32[]{:S(2)}) copy-start(bf16[1040,128]{1,0:T(8,128)(2,1)S(1)} %collective-permute-done.8.refs_6_) | copy-start | bytes 798724
  44.9 8.5 %collective-permute-start.7 = (bf16[1040,128]{1,0:T(8,128)(2,1)S(1)}, bf16[1040,128]{1,0:T(8,128)(2,1)}, u32[]{:S(2)}, u32[]{:S(2)}) collective-permute-start(bf16[1040,128]{1,0:T(8,128)(2,1)S(1)} %collective-permute-done.5.refs_3_), channel_id=1, source_target_pairs={{0,112},{16,0},{32,16},{48,32},{64,48},{80,64},{96,80},{112,96},{1... | collective-permute-start | bytes 798728 | tf_op jit(solution)/shard_map/ppermute | solution.py:383
  50.6 23.3 %copy-start.8 = (bf16[1040,128]{1,0:T(8,128)(2,1)}, bf16[1040,128]{1,0:T(8,128)(2,1)S(1)}, u32[]{:S(2)}) copy-start(bf16[1040,128]{1,0:T(8,128)(2,1)S(1)} %collective-permute-done.13.refs_12_) | copy-start | bytes 798724
  50.6 7.3 %collective-permute-start.9 = (bf16[1040,128]{1,0:T(8,128)(2,1)S(1)}, bf16[1040,128]{1,0:T(8,128)(2,1)}, u32[]{:S(2)}, u32[]{:S(2)}) collective-permute-start(bf16[1040,128]{1,0:T(8,128)(2,1)S(1)} %collective-permute-done.8.refs_6_), channel_id=1, source_target_pairs={{0,16},{16,32},{32,48},{48,64},{64,80},{80,96},{96,112},{112,0},{1... | collective-permute-start | bytes 798728 | tf_op jit(solution)/shard_map/ppermute | solution.py:380
  50.6 13.0 %collective-permute-start.15 = (bf16[1040,128]{1,0:T(8,128)(2,1)S(1)}, bf16[1040,128]{1,0:T(8,128)(2,1)}, u32[]{:S(2)}, u32[]{:S(2)}) collective-permute-start(bf16[1040,128]{1,0:T(8,128)(2,1)S(1)} %collective-permute-done.13.refs_12_), channel_id=1, source_target_pairs={{0,16},{16,32},{32,48},{48,64},{64,80},{80,96},{96,112},{112,0},{1... | collective-permute-start | bytes 798728 | tf_op jit(solution)/shard_map/ppermute | solution.py:384
  50.7 23.2 %copy-start.9 = (bf16[1040,128]{1,0:T(8,128)(2,1)}, bf16[1040,128]{1,0:T(8,128)(2,1)S(1)}, u32[]{:S(2)}) copy-start(bf16[1040,128]{1,0:T(8,128)(2,1)S(1)} %collective-permute-done.14.refs_13_) | copy-start | bytes 798724
  50.7 12.9 %collective-permute-start.16 = (bf16[1040,128]{1,0:T(8,128)(2,1)S(1)}, bf16[1040,128]{1,0:T(8,128)(2,1)}, u32[]{:S(2)}, u32[]{:S(2)}) collective-permute-start(bf16[1040,128]{1,0:T(8,128)(2,1)S(1)} %collective-permute-done.14.refs_13_), channel_id=1, source_target_pairs={{0,112},{16,0},{32,16},{48,32},{64,48},{80,64},{96,80},{112,96},{1... | collective-permute-start | bytes 798728 | tf_op jit(solution)/shard_map/ppermute | solution.py:381
  53.4 20.5 %collective-permute-start.1 = (bf16[2,128,1792]{2,1,0:T(8,128)(2,1)}, bf16[2,128,1792]{2,1,0:T(8,128)(2,1)S(1)}, u32[]{:S(2)}, u32[]{:S(2)}) collective-permute-start(bf16[2,128,1792]{2,1,0:T(8,128)(2,1)} %shard_map.65), channel_id=1, source_target_pairs={{0,128},{128,0},{1,129},{129,1},{2,130},{130,2},{3,131},{131,3},{4... | collective-permute-start | bytes 2752520 | tf_op jit(solution)/shard_map/ppermute | solution.py:375
  69.9 9.3 %collective-permute-start.19 = (f32[2,256,512]{2,1,0:T(8,128)}, f32[2,256,512]{2,1,0:T(8,128)S(1)}, u32[]{:S(2)}, u32[]{:S(2)}) collective-permute-start(f32[2,256,512]{2,1,0:T(8,128)} %shard_map.68), channel_id=1, source_target_pairs={{0,8},{8,0},{1,9},{9,1},{2,10},{10,2},{3,11},{11,3},{4,12},{12,4},... | collective-permute-start | bytes 3145736 | tf_op jit(solution)/shard_map/ppermute | solution.py:387
  80.9 16.4 %all-to-all-start = ((bf16[16,32,512]{2,1,0:T(8,128)(2,1)}), bf16[16,32,512]{2,1,0:T(8,128)(2,1)S(1)}, u32[]{:S(2)}, u32[]{:S(2)}) async-start(bf16[16,32,512]{2,1,0:T(8,128)(2,1)} %shard_map.69), calls=%async_computation | async-start | bytes 1048576 | tf_op jit(solution)/shard_map/all_to_all | solution.py:414
  88.4 25.5 %copy-start.14 = (s32[8]{0:T(128)S(1)}, s32[8]{0:T(128)}, u32[]{:S(2)}) copy-start(s32[8]{0:T(128)} %constant.128) | copy-start | bytes 100
  102.9 41.1 %all-to-all-start.1 = ((bf16[256,16,128]{2,1,0:T(8,128)(2,1)}), bf16[256,16,128]{2,1,0:T(8,128)(2,1)S(1)}, u32[]{:S(2)}, u32[]{:S(2)}) async-start(bf16[256,16,128]{2,1,0:T(8,128)(2,1)} %bitcast.6), calls=%async_computation.1 | async-start | bytes 2097152 | tf_op jit(solution)/shard_map/all_to_all | solution.py:417
  121.6 3.0 %collective-permute-start.20 = (bf16[16,128]{1,0:T(8,128)(2,1)S(1)}, bf16[16,128]{1,0:T(8,128)(2,1)S(1)}, u32[]{:S(2)}, u32[]{:S(2)}) collective-permute-start(bf16[16,128]{1,0:T(8,128)(2,1)S(1)} %concatenate.15), channel_id=1, source_target_pairs={{0,8},{8,0},{1,9},{9,1},{2,10},{10,2},{3,11},{11,3},{4,12},{12,4},... | collective-permute-start | bytes 12296 | tf_op jit(solution)/shard_map/ppermute | solution.py:395
  (7 other events, 48.8 us)
